TPU v7x, 512 devices: a whole 4x8x8 slice. The times are simulated.
512 devices in a mesh: outer: 32 (over z, y_lo), inner: 16 (over y_hi, x, core).
Axes of the slice: x: 4, y: 8 (y_hi: 2, y_lo: 4; y = y_hi * 4 + y_lo), z: 8, core: 2. Of those that a mesh axis runs over, the one named last changes fastest.
Arguments:
- queries: bfloat16 [65536, 1280], P(('outer', 'inner')), may hold values from -1.5 to 1.5
- key_states: bfloat16 [65536, 1280], P(('outer', 'inner')), may hold values from -3 to 3
- value_states: bfloat16 [65536, 1280], P(('outer', 'inner')), may hold values from -4 to 4
- out_grad: bfloat16 [65536, 1280], P(('outer', 'inner')), may hold values from -96 to 96
- log_total: float32 [20, 65536], P(None, ('outer', 'inner')), may hold values from 5 to 8.5
- row_delta: float32 [20, 65536], P(None, ('outer', 'inner')), may hold values from -256 to 256
Outputs:
- query_grad: bfloat16 [65536, 1280], P(('outer', 'inner'))
- key_grad: bfloat16 [65536, 1280], P(('outer', 'inner'))
- value_grad: bfloat16 [65536, 1280], P(('outer', 'inner'))
All inputs are finite; a program needn't handle non-finite values.
Results may differ from a plain program's by a relative error of at most 0.0049.
Values may be sent and summed in bfloat16 or wider, within the bound.
A program may use at most 64 MiB of HBM per device.

v0:
```python
import jax
import jax.numpy as jnp
from jax import lax
from jax.sharding import PartitionSpec as P

HEAD_DIM = 64
OUTER_STEPS = 2
INNER_PASSES = 2


def shifted(block, axis, distance):
    devices = range(lax.axis_size(axis))
    route = [((i - distance) % len(devices), i) for i in devices]
    return lax.ppermute(block, axis, route)


def for_sending(shard):

    def short(part):
        return part.astype(jnp.bfloat16) if part.dtype == jnp.float32 else part

    return jax.tree.map(short, shard)


def pair_terms(query_rows, grad_rows, log_local, delta_local, key_block, value_block):
    token_rows, width_all = query_rows.shape
    head_count = log_local.shape[0]
    head_width = width_all // head_count
    scale = HEAD_DIM ** (-0.5)
    query_heads = query_rows.reshape(token_rows, head_count, head_width)
    grad_heads = grad_rows.reshape(token_rows, head_count, head_width)
    key_heads = key_block.reshape(key_block.shape[0], head_count, head_width)
    value_heads = value_block.reshape(value_block.shape[0], head_count, head_width)
    scores = (
        jnp.einsum("qhd,khd->hqk", query_heads, key_heads, preferred_element_type=jnp.float32)
        * scale
    )
    probs = jnp.exp(scores - log_local[:, :, None])
    probs_low = probs.astype(jnp.bfloat16)
    dprobs = jnp.einsum("qhd,khd->hqk", grad_heads, value_heads, preferred_element_type=jnp.float32)
    score_grad = (probs * (dprobs - delta_local[:, :, None])).astype(jnp.bfloat16)
    query_part = jnp.einsum(
        "hqk,khd->qhd", score_grad, key_heads, preferred_element_type=jnp.float32
    )
    key_part = jnp.einsum(
        "hqk,qhd->khd", score_grad, query_heads, preferred_element_type=jnp.float32
    )
    value_part = jnp.einsum(
        "hqk,qhd->khd", probs_low, grad_heads, preferred_element_type=jnp.float32
    )
    return (
        query_part.reshape(token_rows, width_all),
        key_part.reshape(key_block.shape[0], width_all),
        value_part.reshape(value_block.shape[0], width_all),
    )


def body(queries, key_states, value_states, out_grad, log_total, row_delta):
    token_rows, width_all = queries.shape
    query_sum = jnp.zeros((token_rows, width_all), jnp.float32)
    key_total = jnp.zeros((token_rows, width_all), jnp.float32)
    value_total = jnp.zeros((token_rows, width_all), jnp.float32)
    group_home = (key_states, value_states)
    for outer_step in range(OUTER_STEPS):
        fetched = []
        if outer_step > 0:
            group_home = shifted((group_home[0], group_home[1]), "outer", 1)
        current = group_home
        key_carry = jnp.zeros((token_rows, width_all), jnp.float32)
        value_carry = jnp.zeros((token_rows, width_all), jnp.float32)
        seen_blocks = []
        for inner_pass in range(INNER_PASSES):
            if inner_pass > 0:
                current = jax.tree.map(
                    lambda part, own: part.astype(own.dtype),
                    shifted(for_sending(current), "inner", 1),
                    current,
                )
            if inner_pass > 0:
                key_carry, value_carry = shifted((key_carry, value_carry), "inner", 1)
            seen_blocks.append(current)
            query_part, key_part, value_part = pair_terms(
                queries, out_grad, log_total, row_delta, current[0], current[1]
            )
            query_sum = query_sum + query_part
            key_carry = key_carry + key_part
            value_carry = value_carry + value_part
        key_carry, value_carry = shifted((key_carry, value_carry), "inner", 1 - INNER_PASSES)
        if outer_step > 0:
            key_carry, value_carry = shifted((key_carry, value_carry), "outer", -outer_step)
        key_total = key_total + key_carry
        value_total = value_total + value_carry
    scale = HEAD_DIM ** (-0.5)
    return (
        (query_sum * scale).astype(jnp.bfloat16),
        (key_total * scale).astype(jnp.bfloat16),
        value_total.astype(jnp.bfloat16),
    )


def solution(mesh):
    return jax.shard_map(
        body,
        mesh=mesh,
        in_specs=(
            P(("outer", "inner"), None),
            P(("outer", "inner"), None),
            P(("outer", "inner"), None),
            P(("outer", "inner"), None),
            P(None, ("outer", "inner")),
            P(None, ("outer", "inner")),
        ),
        out_specs=(
            P(("outer", "inner"), None),
            P(("outer", "inner"), None),
            P(("outer", "inner"), None),
        ),
        check_vma=False,
    )
```

profile of v0, /device:TPU:201, one launch (start us, length us, event | category | flops | bytes accessed | tf_op | source)
XLA Modules:
  0.0 198.7 jit_solution(5152767263195161840)
XLA Ops:
  0.7 3.3 %collective-permute-start.2 = (bf16[128,1280]{1,0:T(8,128)(2,1)}, bf16[128,1280]{1,0:T(8,128)(2,1)}, u32[]{:S(2)}, u32[]{:S(2)}) collective-permute-start(bf16[128,1280]{1,0:T(8,128)(2,1)} %param.7), channel_id=1, source_target_pairs={{496,0},{0,16},{16,32},{32,48},{48,64},{64,80},{80,96},{96,112},{1... | collective-permute-start | bytes 983048 | tf_op jit(solution)/shard_map/ppermute | solution.py:14
  4.0 4.0 %collective-permute-start = (bf16[128,1280]{1,0:T(8,128)(2,1)}, bf16[128,1280]{1,0:T(8,128)(2,1)}, u32[]{:S(2)}, u32[]{:S(2)}) collective-permute-start(bf16[128,1280]{1,0:T(8,128)(2,1)} %param.7), channel_id=1, source_target_pairs={{15,0},{0,1},{1,2},{2,3},{3,4},{4,5},{5,6},{6,7},{7,8},{8,9},{9,10... | collective-permute-start | bytes 983048 | tf_op jit(solution)/shard_map/ppermute | solution.py:14
  8.0 3.2 %collective-permute-start.3 = (bf16[128,1280]{1,0:T(8,128)(2,1)}, bf16[128,1280]{1,0:T(8,128)(2,1)}, u32[]{:S(2)}, u32[]{:S(2)}) collective-permute-start(bf16[128,1280]{1,0:T(8,128)(2,1)} %param.8), channel_id=1, source_target_pairs={{496,0},{0,16},{16,32},{32,48},{48,64},{64,80},{80,96},{96,112},{1... | collective-permute-start | bytes 983048 | tf_op jit(solution)/shard_map/ppermute | solution.py:14
  11.2 2.2 %collective-permute-start.1 = (bf16[128,1280]{1,0:T(8,128)(2,1)}, bf16[128,1280]{1,0:T(8,128)(2,1)}, u32[]{:S(2)}, u32[]{:S(2)}) collective-permute-start(bf16[128,1280]{1,0:T(8,128)(2,1)} %param.8), channel_id=1, source_target_pairs={{15,0},{0,1},{1,2},{2,3},{3,4},{4,5},{5,6},{6,7},{7,8},{8,9},{9,10... | collective-permute-start | bytes 983048 | tf_op jit(solution)/shard_map/ppermute | solution.py:14
  13.4 1.2 copy.44
  14.6 1.2 copy.46
  17.7 1.2 fusion.27
  18.8 2.2 %copy.53 = f32[128,1280]{1,0:T(8,128)} copy(f32[128,1280]{0,1:T(8,128)} %bitcast.99) | data formatting | bytes 1310720 | tf_op jit(solution)/shard_map/reshape | solution.py:53
  21.0 3.2 %collective-permute-start.6 = (f32[128,1280]{1,0:T(8,128)}, f32[128,1280]{1,0:T(8,128)}, u32[]{:S(2)}, u32[]{:S(2)}) collective-permute-start(f32[128,1280]{1,0:T(8,128)} %copy.53), channel_id=1, source_target_pairs={{15,0},{0,1},{1,2},{2,3},{3,4},{4,5},{5,6},{6,7},{7,8},{8,9},{9,10... | collective-permute-start | bytes 1966088 | tf_op jit(solution)/shard_map/ppermute | solution.py:14
  24.2 1.2 fusion.24
  25.4 1.4 fusion.26
  27.8 2.2 %collective-permute-start.11 = (f32[128,1280]{1,0:T(8,128)}, f32[128,1280]{1,0:T(8,128)}, u32[]{:S(2)}, u32[]{:S(2)}) collective-permute-start(f32[128,1280]{1,0:T(8,128)} %copy.57), channel_id=1, source_target_pairs={{15,0},{0,1},{1,2},{2,3},{3,4},{4,5},{5,6},{6,7},{7,8},{8,9},{9,10... | collective-permute-start | bytes 1966088 | tf_op jit(solution)/shard_map/ppermute | solution.py:14
  30.0 1.2 copy.47
  32.0 1.9 copy.49
  33.9 1.6 fusion.7
  35.5 1.9 copy.48
  37.4 2.4 %fusion.14 = bf16[20,128,128]{2,1,0:T(8,128)(2,1)} fusion(f32[20,128,128]{2,1,0:T(8,128)S(1)} %fusion.4, bf16[128,20,64]{0,2,1:T(8,128)(2,1)S(1)} %bitcast.75, bf16[128,20,64]{0,2,1:T(8,128)(2,1)} %bitcast.106, f32[20,128]{1,0:T(8,128)S(1)} %copy-done.16), kind=kOutput, calls=%fused_computation.22 | convolution fusion | flops 42926080 | bytes 2631680 | tf_op jit(solution)/shard_map/qhd,khd->hqk/dot_general | solution.py:40
  39.8 1.9 copy.50
  41.7 1.6 fusion.13
  43.3 2.9 %collective-permute-start.4 = (bf16[128,1280]{1,0:T(8,128)(2,1)}, bf16[128,1280]{1,0:T(8,128)(2,1)}, u32[]{:S(2)}, u32[]{:S(2)}) collective-permute-start(bf16[128,1280]{1,0:T(8,128)(2,1)} %collective-permute-done.2), channel_id=1, source_target_pairs={{15,0},{0,1},{1,2},{2,3},{3,4},{4,5},{5,6},{6,7},{7,8},{8,9},{9,10... | collective-permute-start | bytes 983048 | tf_op jit(solution)/shard_map/ppermute | solution.py:14
  46.3 1.2 fusion.20
  47.4 2.3 %collective-permute-start.5 = (bf16[128,1280]{1,0:T(8,128)(2,1)}, bf16[128,1280]{1,0:T(8,128)(2,1)}, u32[]{:S(2)}, u32[]{:S(2)}) collective-permute-start(bf16[128,1280]{1,0:T(8,128)(2,1)} %collective-permute-done.3), channel_id=1, source_target_pairs={{15,0},{0,1},{1,2},{2,3},{3,4},{4,5},{5,6},{6,7},{7,8},{8,9},{9,10... | collective-permute-start | bytes 983048 | tf_op jit(solution)/shard_map/ppermute | solution.py:14
  50.1 1.1 copy.59
  51.1 1.1 copy.55
  52.2 4.8 %collective-permute-start.8 = (f32[128,1280]{1,0:T(8,128)}, f32[128,1280]{1,0:T(8,128)}, u32[]{:S(2)}, u32[]{:S(2)}) collective-permute-start(f32[128,1280]{1,0:T(8,128)} %copy.55), channel_id=1, source_target_pairs={{15,0},{0,1},{1,2},{2,3},{3,4},{4,5},{5,6},{6,7},{7,8},{8,9},{9,10... | collective-permute-start | bytes 1966088 | tf_op jit(solution)/shard_map/ppermute | solution.py:14
  57.0 2.2 %collective-permute-start.13 = (f32[128,1280]{1,0:T(8,128)}, f32[128,1280]{1,0:T(8,128)}, u32[]{:S(2)}, u32[]{:S(2)}) collective-permute-start(f32[128,1280]{1,0:T(8,128)} %copy.59), channel_id=1, source_target_pairs={{15,0},{0,1},{1,2},{2,3},{3,4},{4,5},{5,6},{6,7},{7,8},{8,9},{9,10... | collective-permute-start | bytes 1966088 | tf_op jit(solution)/shard_map/ppermute | solution.py:14
  59.2 1.9 copy.51
  61.1 1.6 fusion.10
  62.7 1.9 copy.52
  64.6 1.6 fusion.12
  67.1 1.2 fusion.30
  68.3 2.2 %copy.56 = f32[128,1280]{1,0:T(8,128)} copy(f32[128,1280]{0,1:T(8,128)} %bitcast.100) | data formatting | bytes 1310720 | tf_op jit(solution)/shard_map/reshape | solution.py:53
  70.5 2.2 %add.40 = f32[128,1280]{1,0:T(8,128)} add(f32[128,1280]{1,0:T(8,128)} %collective-permute-done.8, f32[128,1280]{1,0:T(8,128)} %copy.56) | non-fusion elementwise | flops 163840 | bytes 1966080 | tf_op jit(solution)/shard_map/add | solution.py:86
  72.7 38.1 %collective-permute-start.9 = (f32[128,1280]{1,0:T(8,128)}, f32[128,1280]{1,0:T(8,128)}, u32[]{:S(2)}, u32[]{:S(2)}) collective-permute-start(f32[128,1280]{1,0:T(8,128)} %add.40), channel_id=1, source_target_pairs={{1,0},{2,1},{3,2},{4,3},{5,4},{6,5},{7,6},{8,7},{9,8},{10,9},{11,1... | collective-permute-start | bytes 1966088 | tf_op jit(solution)/shard_map/ppermute | solution.py:14
  110.9 1.2 fusion.22
  112.0 1.2 fusion.18
  113.2 1.3 copy.60
  114.6 2.1 %add.43 = f32[128,1280]{1,0:T(8,128)} add(f32[128,1280]{1,0:T(8,128)} %collective-permute-done.13, f32[128,1280]{1,0:T(8,128)S(1)} %copy.60) | non-fusion elementwise | flops 163840 | bytes 1966080 | tf_op jit(solution)/shard_map/add | solution.py:87
  116.7 5.0 %collective-permute-start.14 = (f32[128,1280]{1,0:T(8,128)}, f32[128,1280]{1,0:T(8,128)}, u32[]{:S(2)}, u32[]{:S(2)}) collective-permute-start(f32[128,1280]{1,0:T(8,128)} %add.43), channel_id=1, source_target_pairs={{1,0},{2,1},{3,2},{4,3},{5,4},{6,5},{7,6},{8,7},{9,8},{10,9},{11,1... | collective-permute-start | bytes 1966088 | tf_op jit(solution)/shard_map/ppermute | solution.py:14
  122.3 2.1 %add.39 = f32[128,1280]{1,0:T(8,128)} add(f32[128,1280]{1,0:T(8,128)} %collective-permute-done.6, f32[128,1280]{1,0:T(8,128)S(1)} %copy.54) | non-fusion elementwise | flops 163840 | bytes 1966080 | tf_op jit(solution)/shard_map/add | solution.py:86
  124.4 2.0 %collective-permute-start.7 = (f32[128,1280]{1,0:T(8,128)}, f32[128,1280]{1,0:T(8,128)}, u32[]{:S(2)}, u32[]{:S(2)}) collective-permute-start(f32[128,1280]{1,0:T(8,128)} %add.39), channel_id=1, source_target_pairs={{1,0},{2,1},{3,2},{4,3},{5,4},{6,5},{7,6},{8,7},{9,8},{10,9},{11,1... | collective-permute-start | bytes 1966088 | tf_op jit(solution)/shard_map/ppermute | solution.py:14
  126.4 1.9 collective-permute-start.10
  129.8 1.2 add.42
  131.0 1.9 collective-permute-start.12
  132.9 1.9 collective-permute-start.15
  137.0 33.0 %collective-permute-done.10 = f32[128,1280]{1,0:T(8,128)} collective-permute-done((f32[128,1280]{1,0:T(8,128)}, f32[128,1280]{1,0:T(8,128)}, u32[]{:S(2)}, u32[]{:S(2)}) %collective-permute-start.10) | collective-permute-done | bytes 655392 | tf_op jit(solution)/shard_map/ppermute | solution.py:14
  169.9 2.1 %multiply_convert_fusion = bf16[128,1280]{1,0:T(8,128)(2,1)} fusion(f32[128,1280]{1,0:T(8,128)} %collective-permute-done.7, f32[128,1280]{1,0:T(8,128)} %collective-permute-done.10), kind=kLoop, calls=%fused_computation.38 | loop fusion | flops 491520 | bytes 1638400 | tf_op jit(solution)/shard_map/convert_element_type | solution.py:96
  172.0 25.9 %collective-permute-done.15 = f32[128,1280]{1,0:T(8,128)S(1)} collective-permute-done((f32[128,1280]{1,0:T(8,128)}, f32[128,1280]{1,0:T(8,128)S(1)}, u32[]{:S(2)}, u32[]{:S(2)}) %collective-permute-start.15) | collective-permute-done | bytes 655392 | tf_op jit(solution)/shard_map/ppermute | solution.py:14
  (63 shorter events, 9.7 us)
Async XLA Ops:
  0.6 15.1 %copy-start.13 = (bf16[128,1280]{1,0:T(8,128)(2,1)S(1)}, bf16[128,1280]{1,0:T(8,128)(2,1)}, u32[]{:S(2)}) copy-start(bf16[128,1280]{1,0:T(8,128)(2,1)} %param.6) | copy-start | bytes 983044
  0.6 15.4 %copy-start.14 = (bf16[128,1280]{1,0:T(8,128)(2,1)S(1)}, bf16[128,1280]{1,0:T(8,128)(2,1)}, u32[]{:S(2)}) copy-start(bf16[128,1280]{1,0:T(8,128)(2,1)} %param.9) | copy-start | bytes 983044
  0.7 15.6 %copy-start.15 = (f32[20,128]{1,0:T(8,128)S(1)}, f32[20,128]{1,0:T(8,128)}, u32[]{:S(2)}) copy-start(f32[20,128]{1,0:T(8,128)} %param.10) | copy-start | bytes 30724
  0.7 31.4 %collective-permute-start.2 = (bf16[128,1280]{1,0:T(8,128)(2,1)}, bf16[128,1280]{1,0:T(8,128)(2,1)}, u32[]{:S(2)}, u32[]{:S(2)}) collective-permute-start(bf16[128,1280]{1,0:T(8,128)(2,1)} %param.7), channel_id=1, source_target_pairs={{496,0},{0,16},{16,32},{32,48},{48,64},{64,80},{80,96},{96,112},{1... | collective-permute-start | bytes 983048 | tf_op jit(solution)/shard_map/ppermute | solution.py:14
  4.0 23.8 %collective-permute-start = (bf16[128,1280]{1,0:T(8,128)(2,1)}, bf16[128,1280]{1,0:T(8,128)(2,1)}, u32[]{:S(2)}, u32[]{:S(2)}) collective-permute-start(bf16[128,1280]{1,0:T(8,128)(2,1)} %param.7), channel_id=1, source_target_pairs={{15,0},{0,1},{1,2},{2,3},{3,4},{4,5},{5,6},{6,7},{7,8},{8,9},{9,10... | collective-permute-start | bytes 983048 | tf_op jit(solution)/shard_map/ppermute | solution.py:14
  8.0 31.9 %collective-permute-start.3 = (bf16[128,1280]{1,0:T(8,128)(2,1)}, bf16[128,1280]{1,0:T(8,128)(2,1)}, u32[]{:S(2)}, u32[]{:S(2)}) collective-permute-start(bf16[128,1280]{1,0:T(8,128)(2,1)} %param.8), channel_id=1, source_target_pairs={{496,0},{0,16},{16,32},{32,48},{48,64},{64,80},{80,96},{96,112},{1... | collective-permute-start | bytes 983048 | tf_op jit(solution)/shard_map/ppermute | solution.py:14
  11.2 24.3 %collective-permute-start.1 = (bf16[128,1280]{1,0:T(8,128)(2,1)}, bf16[128,1280]{1,0:T(8,128)(2,1)}, u32[]{:S(2)}, u32[]{:S(2)}) collective-permute-start(bf16[128,1280]{1,0:T(8,128)(2,1)} %param.8), channel_id=1, source_target_pairs={{15,0},{0,1},{1,2},{2,3},{3,4},{4,5},{5,6},{6,7},{7,8},{8,9},{9,10... | collective-permute-start | bytes 983048 | tf_op jit(solution)/shard_map/ppermute | solution.py:14
  16.0 1.0 copy-start.16
  21.0 101.3 %collective-permute-start.6 = (f32[128,1280]{1,0:T(8,128)}, f32[128,1280]{1,0:T(8,128)}, u32[]{:S(2)}, u32[]{:S(2)}) collective-permute-start(f32[128,1280]{1,0:T(8,128)} %copy.53), channel_id=1, source_target_pairs={{15,0},{0,1},{1,2},{2,3},{3,4},{4,5},{5,6},{6,7},{7,8},{8,9},{9,10... | collective-permute-start | bytes 1966088 | tf_op jit(solution)/shard_map/ppermute | solution.py:14
  25.4 1.4 copy-start.12
  27.8 101.9 %collective-permute-start.11 = (f32[128,1280]{1,0:T(8,128)}, f32[128,1280]{1,0:T(8,128)}, u32[]{:S(2)}, u32[]{:S(2)}) collective-permute-start(f32[128,1280]{1,0:T(8,128)} %copy.57), channel_id=1, source_target_pairs={{15,0},{0,1},{1,2},{2,3},{3,4},{4,5},{5,6},{6,7},{7,8},{8,9},{9,10... | collective-permute-start | bytes 1966088 | tf_op jit(solution)/shard_map/ppermute | solution.py:14
  31.2 2.7 %copy-start.5 = (bf16[128,1280]{0,1:T(8,128)(2,1)}, bf16[128,1280]{0,1:T(8,128)(2,1)S(1)}, u32[]{:S(2)}) copy-start(bf16[128,1280]{0,1:T(8,128)(2,1)S(1)} %copy.47) | copy-start | bytes 983044
  43.3 6.7 %copy-start.1 = (bf16[20,128,128]{2,1,0:T(8,128)(2,1)}, bf16[20,128,128]{2,1,0:T(8,128)(2,1)S(1)}, u32[]{:S(2)}) copy-start(bf16[20,128,128]{2,1,0:T(8,128)(2,1)S(1)} %fusion.13) | copy-start | bytes 1966084
  43.3 13.7 %collective-permute-start.4 = (bf16[128,1280]{1,0:T(8,128)(2,1)}, bf16[128,1280]{1,0:T(8,128)(2,1)}, u32[]{:S(2)}, u32[]{:S(2)}) collective-permute-start(bf16[128,1280]{1,0:T(8,128)(2,1)} %collective-permute-done.2), channel_id=1, source_target_pairs={{15,0},{0,1},{1,2},{2,3},{3,4},{4,5},{5,6},{6,7},{7,8},{8,9},{9,10... | collective-permute-start | bytes 983048 | tf_op jit(solution)/shard_map/ppermute | solution.py:14
  47.4 2.6 %copy-start.11 = (f32[20,128,64]{1,2,0:T(8,128)S(1)}, f32[20,128,64]{1,2,0:T(8,128)}, u32[]{:S(2)}) copy-start(f32[20,128,64]{1,2,0:T(8,128)} %fusion.20) | copy-start | bytes 1966084
  47.4 15.3 %collective-permute-start.5 = (bf16[128,1280]{1,0:T(8,128)(2,1)}, bf16[128,1280]{1,0:T(8,128)(2,1)}, u32[]{:S(2)}, u32[]{:S(2)}) collective-permute-start(bf16[128,1280]{1,0:T(8,128)(2,1)} %collective-permute-done.3), channel_id=1, source_target_pairs={{15,0},{0,1},{1,2},{2,3},{3,4},{4,5},{5,6},{6,7},{7,8},{8,9},{9,10... | collective-permute-start | bytes 983048 | tf_op jit(solution)/shard_map/ppermute | solution.py:14
  52.2 18.2 %collective-permute-start.8 = (f32[128,1280]{1,0:T(8,128)}, f32[128,1280]{1,0:T(8,128)}, u32[]{:S(2)}, u32[]{:S(2)}) collective-permute-start(f32[128,1280]{1,0:T(8,128)} %copy.55), channel_id=1, source_target_pairs={{15,0},{0,1},{1,2},{2,3},{3,4},{4,5},{5,6},{6,7},{7,8},{8,9},{9,10... | collective-permute-start | bytes 1966088 | tf_op jit(solution)/shard_map/ppermute | solution.py:14
  57.0 57.6 %collective-permute-start.13 = (f32[128,1280]{1,0:T(8,128)}, f32[128,1280]{1,0:T(8,128)}, u32[]{:S(2)}, u32[]{:S(2)}) collective-permute-start(f32[128,1280]{1,0:T(8,128)} %copy.59), channel_id=1, source_target_pairs={{15,0},{0,1},{1,2},{2,3},{3,4},{4,5},{5,6},{6,7},{7,8},{8,9},{9,10... | collective-permute-start | bytes 1966088 | tf_op jit(solution)/shard_map/ppermute | solution.py:14
  66.2 0.9 copy-start.3
  72.7 53.7 %collective-permute-start.9 = (f32[128,1280]{1,0:T(8,128)}, f32[128,1280]{1,0:T(8,128)}, u32[]{:S(2)}, u32[]{:S(2)}) collective-permute-start(f32[128,1280]{1,0:T(8,128)} %add.40), channel_id=1, source_target_pairs={{1,0},{2,1},{3,2},{4,3},{5,4},{6,5},{7,6},{8,7},{9,8},{10,9},{11,1... | collective-permute-start | bytes 1966088 | tf_op jit(solution)/shard_map/ppermute | solution.py:14
  114.6 7.1 %copy-start = (bf16[20,128,128]{2,1,0:T(8,128)(2,1)S(1)}, bf16[20,128,128]{2,1,0:T(8,128)(2,1)}, u32[]{:S(2)}) copy-start(bf16[20,128,128]{2,1,0:T(8,128)(2,1)} %fusion.14) | copy-start | bytes 1966084
  116.7 16.2 %collective-permute-start.14 = (f32[128,1280]{1,0:T(8,128)}, f32[128,1280]{1,0:T(8,128)}, u32[]{:S(2)}, u32[]{:S(2)}) collective-permute-start(f32[128,1280]{1,0:T(8,128)} %add.43), channel_id=1, source_target_pairs={{1,0},{2,1},{3,2},{4,3},{5,4},{6,5},{7,6},{8,7},{9,8},{10,9},{11,1... | collective-permute-start | bytes 1966088 | tf_op jit(solution)/shard_map/ppermute | solution.py:14
  122.2 6.1 %copy-start.6 = (bf16[128,1280]{0,1:T(8,128)(2,1)S(1)}, bf16[128,1280]{0,1:T(8,128)(2,1)}, u32[]{:S(2)}) copy-start(bf16[128,1280]{0,1:T(8,128)(2,1)} %copy-done.5) | copy-start | bytes 983044
  122.2 6.1 %copy-start.9 = (f32[20,128,64]{1,2,0:T(8,128)S(1)}, f32[20,128,64]{1,2,0:T(8,128)}, u32[]{:S(2)}) copy-start(f32[20,128,64]{1,2,0:T(8,128)} %fusion.26) | copy-start | bytes 1966084
  124.3 4.6 %copy-start.10 = (f32[20,128,64]{1,2,0:T(8,128)S(1)}, f32[20,128,64]{1,2,0:T(8,128)}, u32[]{:S(2)}) copy-start(f32[20,128,64]{1,2,0:T(8,128)} %fusion.22) | copy-start | bytes 1966084
  124.3 4.8 %copy-start.2 = (bf16[20,128,128]{2,1,0:T(8,128)(2,1)S(1)}, bf16[20,128,128]{2,1,0:T(8,128)(2,1)}, u32[]{:S(2)}) copy-start(bf16[20,128,128]{2,1,0:T(8,128)(2,1)} %copy-done.1) | copy-start | bytes 1966084
  124.3 4.8 %copy-start.7 = (bf16[128,1280]{0,1:T(8,128)(2,1)S(1)}, bf16[128,1280]{0,1:T(8,128)(2,1)}, u32[]{:S(2)}) copy-start(bf16[128,1280]{0,1:T(8,128)(2,1)} %copy.49) | copy-start | bytes 983044
  124.4 12.6 %collective-permute-start.7 = (f32[128,1280]{1,0:T(8,128)}, f32[128,1280]{1,0:T(8,128)}, u32[]{:S(2)}, u32[]{:S(2)}) collective-permute-start(f32[128,1280]{1,0:T(8,128)} %add.39), channel_id=1, source_target_pairs={{1,0},{2,1},{3,2},{4,3},{5,4},{6,5},{7,6},{8,7},{9,8},{10,9},{11,1... | collective-permute-start | bytes 1966088 | tf_op jit(solution)/shard_map/ppermute | solution.py:14
  126.4 43.5 %collective-permute-start.10 = (f32[128,1280]{1,0:T(8,128)}, f32[128,1280]{1,0:T(8,128)}, u32[]{:S(2)}, u32[]{:S(2)}) collective-permute-start(f32[128,1280]{1,0:T(8,128)} %collective-permute-done.9), channel_id=1, source_target_pairs={{16,0},{32,16},{48,32},{64,48},{80,64},{96,80},{112,96},{128,112},... | collective-permute-start | bytes 1966088 | tf_op jit(solution)/shard_map/ppermute | solution.py:14
  129.7 5.1 %copy-start.4 = (bf16[20,128,128]{2,1,0:T(8,128)(2,1)S(1)}, bf16[20,128,128]{2,1,0:T(8,128)(2,1)}, u32[]{:S(2)}) copy-start(bf16[20,128,128]{2,1,0:T(8,128)(2,1)} %copy-done.3) | copy-start | bytes 1966084
  129.7 5.1 %copy-start.8 = (bf16[128,1280]{0,1:T(8,128)(2,1)S(1)}, bf16[128,1280]{0,1:T(8,128)(2,1)}, u32[]{:S(2)}) copy-start(bf16[128,1280]{0,1:T(8,128)(2,1)} %copy.51) | copy-start | bytes 983044
  131.0 41.0 %collective-permute-start.12 = (f32[128,1280]{1,0:T(8,128)S(1)}, f32[128,1280]{1,0:T(8,128)S(1)}, u32[]{:S(2)}, u32[]{:S(2)}) collective-permute-start(f32[128,1280]{1,0:T(8,128)S(1)} %add.42), channel_id=1, source_target_pairs={{1,0},{2,1},{3,2},{4,3},{5,4},{6,5},{7,6},{8,7},{9,8},{10,9},{11,1... | collective-permute-start | bytes 1966088 | tf_op jit(solution)/shard_map/ppermute | solution.py:14
  132.9 65.0 %collective-permute-start.15 = (f32[128,1280]{1,0:T(8,128)}, f32[128,1280]{1,0:T(8,128)S(1)}, u32[]{:S(2)}, u32[]{:S(2)}) collective-permute-start(f32[128,1280]{1,0:T(8,128)} %collective-permute-done.14), channel_id=1, source_target_pairs={{16,0},{32,16},{48,32},{64,48},{80,64},{96,80},{112,96},{128,112},... | collective-permute-start | bytes 1966088 | tf_op jit(solution)/shard_map/ppermute | solution.py:14
where the time goes:
time: 200 us; the launch traced here: 199 us
  starting transfers between devices  81.2 us (41%)
  waiting for transfers between devices  59.5 us (30%)
  local copies, waits for them, and re-layouts  24.6 us (12%)
  matrix products  21.7 us (11%)
  other arithmetic  10.5 us (5%)
    ppermute x16, starting transfers between devices, shifted(): return lax.ppermute(block, axis, route)  81.2 us
    ppermute x16, waiting for transfers between devices, shifted(): return lax.ppermute(block, axis, route)  59.5 us
    ppermute x6, local copies, waits for them, and re-layouts, shifted(): return lax.ppermute(block, axis, route)  10.6 us
    dot_general x4, matrix products, pair_terms(): jnp.einsum('qhd,khd->hqk', grad_heads, value_heads, preferred_element_typ...  6.26 us
    reshape x4, local copies, waits for them, and re-layouts, pair_terms(): key_part.reshape(key_block.shape[0], width_all)  5.72 us
    dot_general x4, matrix products, pair_terms(): jnp.einsum('qhd,khd->hqk', query_heads, key_heads, preferred_element_type...  4.75 us
    dot_general x4, matrix products, pair_terms(): jnp.einsum('hqk,qhd->khd', probs_low, grad_heads, preferred_element_type=...  4.69 us
    unnamed x39, local copies, waits for them, and re-layouts  4.6 us
  transfers between devices with their start and end apart: 16, of which 3 were waited for; matrix products, arithmetic and copies ran while one was open for 28% of the time, Pallas kernels for 0%

commit v1 on v0

v1 whole, which is shorter than its diff:
```python
import functools
import math

import jax
import jax.numpy as jnp
from jax import lax
from jax.experimental import pallas as pl
from jax.experimental.pallas import tpu as pltpu
from jax.sharding import PartitionSpec as P

HEAD_DIM = 64
SCALE = HEAD_DIM ** (-0.5)
LOG2E = math.log2(math.e)
LANES = 128
MESH = pl.DeviceIdType.MESH
NT = (((1,), (1,)), ((), ()))
NN = (((1,), (0,)), ((), ()))
TN = (((0,), (0,)), ((), ()))


def mm(a, b, dims):
    return lax.dot_general(a, b, dims, preferred_element_type=jnp.float32)


def kernel(
    n_outer, n_inner, chunks,
    q_hbm, k_hbm, v_hbm, g_hbm, log_hbm, delta_hbm,
    dq_hbm, dk_hbm, dv_hbm,
    qg, kv, stats, dq_own, dkv_own, dq_send, dkv_send, dq_recv, dkv_recv, out,
    stage_sem, stat_sem, qg_send_sem, qg_recv_sem, kv_send_sem, kv_recv_sem,
    st_send_sem, st_recv_sem, dq_send_sem, dq_recv_sem, dkv_send_sem, dkv_recv_sem, out_sem,
):
    o, i = lax.axis_index("outer"), lax.axis_index("inner")
    up = (lax.rem(o + 1, n_outer), i)
    down = (lax.rem(o + n_outer - 1, n_outer), i)
    right = (o, lax.rem(i + 1, n_inner))
    left = (o, lax.rem(i + n_inner - 1, n_inner))

    def columns(c):
        return pl.ds(pl.multiple_of(c * LANES, LANES), LANES)

    def stage(c):
        sources = ((q_hbm, qg, 0), (g_hbm, qg, 1), (k_hbm, kv, 0), (v_hbm, kv, 1))
        return [
            pltpu.make_async_copy(src.at[:, columns(c)], dst.at[c, 0, at], stage_sem.at[c, n])
            for n, (src, dst, at) in enumerate(sources)
        ]

    def remote(src, dst, send, recv, device):
        return pltpu.make_async_remote_copy(
            src_ref=src, dst_ref=dst, send_sem=send, recv_sem=recv,
            device_id=device, device_id_type=MESH,
        )

    def send_qg(c):
        return remote(qg.at[c, 0], qg.at[c, 1], qg_send_sem.at[c], qg_recv_sem.at[c], down)

    def send_kv(c):
        return remote(kv.at[c, 0], kv.at[c, 1], kv_send_sem.at[c], kv_recv_sem.at[c], right)

    def send_stats(n):
        return remote(stats.at[0, n], stats.at[1, n], st_send_sem.at[n], st_recv_sem.at[n], down)

    def send_dq(c):
        return remote(dq_send.at[c], dq_recv.at[c], dq_send_sem.at[c], dq_recv_sem.at[c], up)

    def send_dkv(c):
        return remote(dkv_send.at[c], dkv_recv.at[c], dkv_send_sem.at[c], dkv_recv_sem.at[c], left)

    def write(c):
        return [
            pltpu.make_async_copy(out.at[n, c], dst.at[:, columns(c)], out_sem.at[c, n])
            for n, dst in enumerate((dq_hbm, dk_hbm, dv_hbm))
        ]

    stat_copies = [
        pltpu.make_async_copy(src, stats.at[0, n], stat_sem.at[n])
        for n, src in enumerate((log_hbm, delta_hbm))
    ]
    for copy in stat_copies:
        copy.start()

    @pl.loop(0, chunks)
    def _(c):
        for copy in stage(c):
            copy.start()

    barrier = pltpu.get_barrier_semaphore()
    for device in (up, down, right, left):
        pl.semaphore_signal(barrier, inc=1, device_id=device, device_id_type=MESH)
    pl.semaphore_wait(barrier, 4)

    for n, copy in enumerate(stat_copies):
        copy.wait()
        send_stats(n).start()

    @pl.loop(0, chunks)
    def _(c):
        for copy in stage(c):
            copy.wait()
        send_qg(c).start()
        send_kv(c).start()

    for n in range(2):
        send_stats(n).wait_recv()

    first_head = lax.broadcasted_iota(jnp.int32, (1, LANES), 1) < HEAD_DIM

    @pl.loop(0, chunks)
    def _(c):
        send_qg(c).wait_recv()
        send_kv(c).wait_recv()
        queries = jnp.concatenate([qg[c, 0, 0], qg[c, 1, 0]], axis=0)
        grads = jnp.concatenate([qg[c, 0, 1], qg[c, 1, 1]], axis=0)
        keys = jnp.concatenate([kv[c, 0, 0], kv[c, 1, 0]], axis=0)
        values = jnp.concatenate([kv[c, 0, 1], kv[c, 1, 1]], axis=0)
        dq = None
        dks, dvs = [], []
        for head in range(2):
            mine = first_head if head == 0 else jnp.logical_not(first_head)
            row = 2 * c + head
            logs = jnp.concatenate([stats[0, 0, pl.ds(row, 1), :], stats[1, 0, pl.ds(row, 1), :]], axis=1)
            deltas = jnp.concatenate([stats[0, 1, pl.ds(row, 1), :], stats[1, 1, pl.ds(row, 1), :]], axis=1)
            keys_h = jnp.where(mine, keys, jnp.zeros_like(keys))
            values_h = jnp.where(mine, values, jnp.zeros_like(values))
            scores = mm(keys_h, queries, NT)
            probs = jnp.exp2(scores * (SCALE * LOG2E) - logs * LOG2E)
            dprobs = mm(values_h, grads, NT)
            score_grad = (probs * (dprobs - deltas)).astype(jnp.bfloat16)
            dvs.append(mm(probs.astype(jnp.bfloat16), grads, NN))
            dks.append(mm(score_grad, queries, NN))
            part = mm(score_grad, keys_h, TN)
            dq = part if dq is None else dq + part
        dk = jnp.where(first_head, dks[0], dks[1]) * SCALE
        dv = jnp.where(first_head, dvs[0], dvs[1])
        dq = dq * SCALE
        rows = dq.shape[0] // 2
        dq_send[c] = dq[rows:].astype(jnp.bfloat16)
        send_dq(c).start()
        dkv_send[c, 0] = dk[rows:].astype(jnp.bfloat16)
        dkv_send[c, 1] = dv[rows:].astype(jnp.bfloat16)
        send_dkv(c).start()
        dq_own[c] = dq[:rows]
        dkv_own[c, 0] = dk[:rows]
        dkv_own[c, 1] = dv[:rows]

    @pl.loop(0, chunks)
    def _(c):
        send_dq(c).wait_recv()
        out[0, c] = (dq_own[c] + dq_recv[c].astype(jnp.float32)).astype(jnp.bfloat16)
        send_dkv(c).wait_recv()
        for n in range(2):
            total = dkv_own[c, n] + dkv_recv[c, n].astype(jnp.float32)
            out[1 + n, c] = total.astype(jnp.bfloat16)
        for copy in write(c):
            copy.start()

    for n in range(2):
        send_stats(n).wait_send()

    @pl.loop(0, chunks)
    def _(c):
        send_qg(c).wait_send()
        send_kv(c).wait_send()
        send_dq(c).wait_send()
        send_dkv(c).wait_send()
        for copy in write(c):
            copy.wait()


def body(queries, key_states, value_states, out_grad, log_total, row_delta):
    rows, width = queries.shape
    heads = log_total.shape[0]
    chunks = width // LANES
    dma = pltpu.SemaphoreType.DMA
    low, full = jnp.bfloat16, jnp.float32
    block = jax.ShapeDtypeStruct((rows, width), low)
    return pl.pallas_call(
        functools.partial(
            kernel, lax.axis_size("outer"), lax.axis_size("inner"), chunks
        ),
        out_shape=(block, block, block),
        in_specs=[pl.BlockSpec(memory_space=pl.ANY)] * 6,
        out_specs=[pl.BlockSpec(memory_space=pl.ANY)] * 3,
        scratch_shapes=[
            pltpu.VMEM((chunks, 2, 2, rows, LANES), low),
            pltpu.VMEM((chunks, 2, 2, rows, LANES), low),
            pltpu.VMEM((2, 2, heads, rows), full),
            pltpu.VMEM((chunks, rows, LANES), full),
            pltpu.VMEM((chunks, 2, rows, LANES), full),
            pltpu.VMEM((chunks, rows, LANES), low),
            pltpu.VMEM((chunks, 2, rows, LANES), low),
            pltpu.VMEM((chunks, rows, LANES), low),
            pltpu.VMEM((chunks, 2, rows, LANES), low),
            pltpu.VMEM((3, chunks, rows, LANES), low),
            dma((chunks, 4)), dma((2,)),
            dma((chunks,)), dma((chunks,)), dma((chunks,)), dma((chunks,)),
            dma((2,)), dma((2,)),
            dma((chunks,)), dma((chunks,)), dma((chunks,)), dma((chunks,)),
            dma((chunks, 3)),
        ],
        compiler_params=pltpu.CompilerParams(
            collective_id=0, has_side_effects=True, vmem_limit_bytes=40 * 2**20
        ),
        cost_estimate=pl.CostEstimate(
            flops=40 * rows * rows * width, bytes_accessed=14 * rows * width,
            transcendentals=4 * heads * rows * rows,
        ),
        name="window_backward",
    )(queries, key_states, value_states, out_grad, log_total, row_delta)


def solution(mesh):
    tokens = P(("outer", "inner"), None)
    stats = P(None, ("outer", "inner"))
    return jax.shard_map(
        body,
        mesh=mesh,
        in_specs=(tokens, tokens, tokens, tokens, stats, stats),
        out_specs=(tokens, tokens, tokens),
        check_vma=False,
    )
```

time: 200 us -> 62.2 us (0.31)
  the two profiles are of different devices: /device:TPU:201 before, /device:TPU:7 now
where the time goes in v1:
time: 62.2 us; the launch traced here: 61.8 us
  Pallas kernels  53.7 us (86%)
  local copies, waits for them, and re-layouts  7.47 us (12%)
  between operations  0.65 us (1%)
    pallas_call x1, Pallas kernels, body(): pl.pallas_call(functools.partial(kernel, lax.axis_size('outer'), lax.axis...  53.7 us
    unnamed x15, local copies, waits for them, and re-layouts  7.47 us

profile of v1, /device:TPU:7, one launch (start us, length us, event | category | flops | bytes accessed | tf_op | source)
XLA Modules:
  0.0 61.8 jit_solution(7781562020401621881)
XLA Ops:
  0.6 0.0 copy-start
  0.6 1.0 %copy-done = bf16[128,1280]{1,0:T(8,128)(2,1)S(1)} copy-done((bf16[128,1280]{1,0:T(8,128)(2,1)S(1)}, bf16[128,1280]{1,0:T(8,128)(2,1)}, u32[]{:S(2)}) %copy-start) | copy-done | bytes 327704
  1.6 0.0 copy-start.1
  1.6 1.0 %copy-done.1 = bf16[128,1280]{1,0:T(8,128)(2,1)S(1)} copy-done((bf16[128,1280]{1,0:T(8,128)(2,1)S(1)}, bf16[128,1280]{1,0:T(8,128)(2,1)}, u32[]{:S(2)}) %copy-start.1) | copy-done | bytes 327704
  2.6 0.0 copy-start.2
  2.6 1.0 %copy-done.2 = bf16[128,1280]{1,0:T(8,128)(2,1)S(1)} copy-done((bf16[128,1280]{1,0:T(8,128)(2,1)S(1)}, bf16[128,1280]{1,0:T(8,128)(2,1)}, u32[]{:S(2)}) %copy-start.2) | copy-done | bytes 327704
  3.6 0.0 copy-start.3
  3.6 1.0 %copy-done.3 = bf16[128,1280]{1,0:T(8,128)(2,1)S(1)} copy-done((bf16[128,1280]{1,0:T(8,128)(2,1)S(1)}, bf16[128,1280]{1,0:T(8,128)(2,1)}, u32[]{:S(2)}) %copy-start.3) | copy-done | bytes 327704
  4.5 0.0 copy-start.4
  4.5 0.7 %copy-done.4 = f32[20,128]{1,0:T(8,128)S(1)} copy-done((f32[20,128]{1,0:T(8,128)S(1)}, f32[20,128]{1,0:T(8,128)}, u32[]{:S(2)}) %copy-start.4) | copy-done | bytes 10264
  5.2 0.0 copy-start.5
  5.2 0.7 %copy-done.5 = f32[20,128]{1,0:T(8,128)S(1)} copy-done((f32[20,128]{1,0:T(8,128)S(1)}, f32[20,128]{1,0:T(8,128)}, u32[]{:S(2)}) %copy-start.5) | copy-done | bytes 10264
  5.9 53.7 %window_backward.1 = (bf16[128,1280]{1,0:T(8,128)(2,1)S(1)}, bf16[128,1280]{1,0:T(8,128)(2,1)S(1)}, bf16[128,1280]{1,0:T(8,128)(2,1)S(1)}) custom-call(bf16[128,1280]{1,0:T(8,128)(2,1)S(1)} %copy-done, bf16[128,1280]{1,0:T(8,128)(2,1)S(1)} %copy-done.1, bf16[128,1280]{1,0:T(8,128)(2,1)S(1)} %copy-done.2, bf16[128,1280]{1,0:T(8,128)(2,1)S(1)} %copy-done.3, ...), custom_call_target="tpu_custom_call" | custom-call | flops 838860800 | bytes 2293760 | tf_op jit(solution)/shard_map/window_backward/pallas_call | solution.py:178
  59.7 0.7 %copy.12 = bf16[128,1280]{1,0:T(8,128)(2,1)} copy(bf16[128,1280]{1,0:T(8,128)(2,1)S(1)} %get-tuple-element.6) | data formatting | bytes 655360
  60.4 0.7 %copy.13 = bf16[128,1280]{1,0:T(8,128)(2,1)} copy(bf16[128,1280]{1,0:T(8,128)(2,1)S(1)} %get-tuple-element.7) | data formatting | bytes 655360
  61.1 0.7 %copy.14 = bf16[128,1280]{1,0:T(8,128)(2,1)} copy(bf16[128,1280]{1,0:T(8,128)(2,1)S(1)} %get-tuple-element.8) | data formatting | bytes 655360
Async XLA Ops:
  0.6 1.0 %copy-start = (bf16[128,1280]{1,0:T(8,128)(2,1)S(1)}, bf16[128,1280]{1,0:T(8,128)(2,1)}, u32[]{:S(2)}) copy-start(bf16[128,1280]{1,0:T(8,128)(2,1)} %q_hbm.1) | copy-start | bytes 983044
  1.6 1.0 %copy-start.1 = (bf16[128,1280]{1,0:T(8,128)(2,1)S(1)}, bf16[128,1280]{1,0:T(8,128)(2,1)}, u32[]{:S(2)}) copy-start(bf16[128,1280]{1,0:T(8,128)(2,1)} %k_hbm.1) | copy-start | bytes 983044
  2.6 1.0 %copy-start.2 = (bf16[128,1280]{1,0:T(8,128)(2,1)S(1)}, bf16[128,1280]{1,0:T(8,128)(2,1)}, u32[]{:S(2)}) copy-start(bf16[128,1280]{1,0:T(8,128)(2,1)} %v_hbm.1) | copy-start | bytes 983044
  3.6 1.0 %copy-start.3 = (bf16[128,1280]{1,0:T(8,128)(2,1)S(1)}, bf16[128,1280]{1,0:T(8,128)(2,1)}, u32[]{:S(2)}) copy-start(bf16[128,1280]{1,0:T(8,128)(2,1)} %g_hbm.1) | copy-start | bytes 983044
  4.5 0.7 %copy-start.4 = (f32[20,128]{1,0:T(8,128)S(1)}, f32[20,128]{1,0:T(8,128)}, u32[]{:S(2)}) copy-start(f32[20,128]{1,0:T(8,128)} %log_hbm.1) | copy-start | bytes 30724
  5.2 0.7 %copy-start.5 = (f32[20,128]{1,0:T(8,128)S(1)}, f32[20,128]{1,0:T(8,128)}, u32[]{:S(2)}) copy-start(f32[20,128]{1,0:T(8,128)} %delta_hbm.1) | copy-start | bytes 30724

commit v2 on v1

--- a/solution.py
+++ b/solution.py
@@ -12,6 +12,7 @@
 SCALE = HEAD_DIM ** (-0.5)
 LOG2E = math.log2(math.e)
 LANES = 128
+RUN = 8
 MESH = pl.DeviceIdType.MESH
 NT = (((1,), (1,)), ((), ()))
 NN = (((1,), (0,)), ((), ()))
@@ -26,9 +27,10 @@
     n_outer, n_inner, chunks,
     q_hbm, k_hbm, v_hbm, g_hbm, log_hbm, delta_hbm,
     dq_hbm, dk_hbm, dv_hbm,
-    qg, kv, stats, dq_own, dkv_own, dq_send, dkv_send, dq_recv, dkv_recv, out,
+    qg, kv, relay, stats, dq_own, dkv_own, dq_send, dkv_send, dq_recv, dkv_recv, out,
     stage_sem, stat_sem, qg_send_sem, qg_recv_sem, kv_send_sem, kv_recv_sem,
     st_send_sem, st_recv_sem, dq_send_sem, dq_recv_sem, dkv_send_sem, dkv_recv_sem, out_sem,
+    relay_send_sem, relay_recv_sem,
 ):
     o, i = lax.axis_index("outer"), lax.axis_index("inner")
     up = (lax.rem(o + 1, n_outer), i)
@@ -36,6 +38,19 @@
     right = (o, lax.rem(i + 1, n_inner))
     left = (o, lax.rem(i + n_inner - 1, n_inner))
 
+    place = lax.rem(i, RUN)
+    sends_keys, sends_sums = place == RUN - 1, place == 0
+    relays_keys, relays_sums = place == RUN - 3, place == 2
+    relays = jnp.logical_or(relays_keys, relays_sums)
+    ends = jnp.logical_or(sends_keys, sends_sums)
+
+    def along(distance):
+        return (o, lax.rem(i + (distance + n_inner), n_inner))
+
+    partners = (
+        (sends_keys, (-2, 3)), (sends_sums, (-3, 2)), (relays_keys, (2, 3)), (relays_sums, (-2, -3)),
+    )
+
     def columns(c):
         return pl.ds(pl.multiple_of(c * LANES, LANES), LANES)
 
@@ -58,6 +73,14 @@
     def send_kv(c):
         return remote(kv.at[c, 0], kv.at[c, 1], kv_send_sem.at[c], kv_recv_sem.at[c], right)
 
+    def send_kv_relay(c):
+        return remote(kv.at[c, 0], relay.at[c // 2], kv_send_sem.at[c], relay_recv_sem.at[c // 2], along(-2))
+
+    def pass_kv(c):
+        return remote(
+            relay.at[c // 2], kv.at[c, 1], relay_send_sem.at[c // 2], kv_recv_sem.at[c], along(3)
+        )
+
     def send_stats(n):
         return remote(stats.at[0, n], stats.at[1, n], st_send_sem.at[n], st_recv_sem.at[n], down)
 
@@ -66,6 +89,25 @@
 
     def send_dkv(c):
         return remote(dkv_send.at[c], dkv_recv.at[c], dkv_send_sem.at[c], dkv_recv_sem.at[c], left)
+
+    def send_dkv_relay(c):
+        return remote(
+            dkv_send.at[c], relay.at[c // 2], dkv_send_sem.at[c], relay_recv_sem.at[c // 2], along(2)
+        )
+
+    def pass_dkv(c):
+        return remote(
+            relay.at[c // 2], dkv_recv.at[c], relay_send_sem.at[c // 2], dkv_recv_sem.at[c], along(-3)
+        )
+
+    def either(condition, one, other):
+        @pl.when(condition)
+        def _():
+            one.start()
+
+        @pl.when(jnp.logical_not(condition))
+        def _():
+            other.start()
 
     def write(c):
         return [
@@ -88,7 +130,12 @@
     barrier = pltpu.get_barrier_semaphore()
     for device in (up, down, right, left):
         pl.semaphore_signal(barrier, inc=1, device_id=device, device_id_type=MESH)
-    pl.semaphore_wait(barrier, 4)
+    for role, distances in partners:
+        @pl.when(role)
+        def _():
+            for distance in distances:
+                pl.semaphore_signal(barrier, inc=1, device_id=along(distance), device_id_type=MESH)
+    pl.semaphore_wait(barrier, 4 + 2 * jnp.logical_or(relays, ends).astype(jnp.int32))
 
     for n, copy in enumerate(stat_copies):
         copy.wait()
@@ -99,10 +146,22 @@
         for copy in stage(c):
             copy.wait()
         send_qg(c).start()
-        send_kv(c).start()
+        odd = lax.rem(c, 2) == 1
+        either(jnp.logical_and(sends_keys, odd), send_kv_relay(c), send_kv(c))
 
     for n in range(2):
         send_stats(n).wait_recv()
+
+    @pl.when(relays_keys)
+    def _():
+        @pl.loop(0, chunks // 2)
+        def _(pair):
+            send_kv_relay(2 * pair + 1).wait_recv()
+            pass_kv(2 * pair + 1).start()
+
+    def relay_sums(c):
+        send_dkv_relay(c).wait_recv()
+        pass_dkv(c).start()
 
     first_head = lax.broadcasted_iota(jnp.int32, (1, LANES), 1) < HEAD_DIM
 
@@ -139,10 +198,20 @@
         send_dq(c).start()
         dkv_send[c, 0] = dk[rows:].astype(jnp.bfloat16)
         dkv_send[c, 1] = dv[rows:].astype(jnp.bfloat16)
-        send_dkv(c).start()
+        odd = lax.rem(c, 2) == 1
+        either(jnp.logical_and(sends_sums, odd), send_dkv_relay(c), send_dkv(c))
+
+        @pl.when(jnp.logical_and(relays_sums, jnp.logical_and(odd, c > 2)))
+        def _():
+            relay_sums(c - 2)
+
         dq_own[c] = dq[:rows]
         dkv_own[c, 0] = dk[:rows]
         dkv_own[c, 1] = dv[:rows]
+
+    @pl.when(relays_sums)
+    def _():
+        relay_sums(chunks - 1)
 
     @pl.loop(0, chunks)
     def _(c):
@@ -157,6 +226,12 @@
 
     for n in range(2):
         send_stats(n).wait_send()
+
+    @pl.when(relays)
+    def _():
+        @pl.loop(0, chunks // 2)
+        def _(pair):
+            pass_kv(2 * pair + 1).wait_send()
 
     @pl.loop(0, chunks)
     def _(c):
@@ -185,6 +260,7 @@
         scratch_shapes=[
             pltpu.VMEM((chunks, 2, 2, rows, LANES), low),
             pltpu.VMEM((chunks, 2, 2, rows, LANES), low),
+            pltpu.VMEM((chunks // 2, 2, rows, LANES), low),
             pltpu.VMEM((2, 2, heads, rows), full),
             pltpu.VMEM((chunks, rows, LANES), full),
             pltpu.VMEM((chunks, 2, rows, LANES), full),
@@ -198,9 +274,10 @@
             dma((2,)), dma((2,)),
             dma((chunks,)), dma((chunks,)), dma((chunks,)), dma((chunks,)),
             dma((chunks, 3)),
+            dma((chunks // 2,)), dma((chunks // 2,)),
         ],
         compiler_params=pltpu.CompilerParams(
-            collective_id=0, has_side_effects=True, vmem_limit_bytes=40 * 2**20
+            collective_id=0, has_side_effects=True, vmem_limit_bytes=60 * 2**20
         ),
         cost_estimate=pl.CostEstimate(
             flops=40 * rows * rows * width, bytes_accessed=14 * rows * width,

time: 62.2 us -> 59.7 us (0.960)
  the two profiles are of different devices: /device:TPU:7 before, /device:TPU:1 now
where the time goes in v2:
time: 59.7 us; the launch traced here: 59.4 us
  Pallas kernels  55.2 us (92%)
  local copies, waits for them, and re-layouts  3.58 us (6%)
  between operations  0.65 us (1%)
    pallas_call x1, Pallas kernels, body(): pl.pallas_call(functools.partial(kernel, lax.axis_size('outer'), lax.axis...  55.2 us
    unnamed x7, local copies, waits for them, and re-layouts  3.58 us

profile of v2, /device:TPU:1, one launch (start us, length us, event | category | flops | bytes accessed | tf_op | source)
XLA Modules:
  0.0 59.4 jit_solution(9630594954892858537)
XLA Ops:
  0.6 55.2 %window_backward.1 = (bf16[128,1280]{1,0:T(8,128)(2,1)}, bf16[128,1280]{1,0:T(8,128)(2,1)}, bf16[128,1280]{1,0:T(8,128)(2,1)}) custom-call(bf16[128,1280]{1,0:T(8,128)(2,1)} %q_hbm.1, bf16[128,1280]{1,0:T(8,128)(2,1)} %k_hbm.1, bf16[128,1280]{1,0:T(8,128)(2,1)} %v_hbm.1, bf16[128,1280]{1,0:T(8,128)(2,1)} %g_hbm.1, f32[20,128]{1,0:T(8,128)} %log_hbm.1, ...), custom_call_target="tpu_custom_call" | custom-call | flops 838860800 | bytes 2293760 | tf_op jit(solution)/shard_map/window_backward/pallas_call | solution.py:253
  55.8 0.0 copy-start.1
  55.8 1.8 %copy.12 = bf16[128,1280]{1,0:T(8,128)(2,1)} copy(bf16[128,1280]{1,0:T(8,128)(2,1)} %get-tuple-element.6) | data formatting | bytes 655360
  57.6 0.0 copy-done.1
  57.6 0.0 copy-start
  57.6 0.7 %copy.13 = bf16[128,1280]{1,0:T(8,128)(2,1)} copy(bf16[128,1280]{1,0:T(8,128)(2,1)S(1)} %copy-done.1) | data formatting | bytes 655360
  58.3 0.4 copy-done
  58.7 0.7 %copy.14 = bf16[128,1280]{1,0:T(8,128)(2,1)} copy(bf16[128,1280]{1,0:T(8,128)(2,1)S(1)} %copy-done) | data formatting | bytes 655360
Async XLA Ops:
  55.8 1.8 %copy-start.1 = (bf16[128,1280]{1,0:T(8,128)(2,1)S(1)}, bf16[128,1280]{1,0:T(8,128)(2,1)}, u32[]{:S(2)}) copy-start(bf16[128,1280]{1,0:T(8,128)(2,1)} %get-tuple-element.7) | copy-start | bytes 983044
  57.6 1.1 %copy-start = (bf16[128,1280]{1,0:T(8,128)(2,1)S(1)}, bf16[128,1280]{1,0:T(8,128)(2,1)}, u32[]{:S(2)}) copy-start(bf16[128,1280]{1,0:T(8,128)(2,1)} %get-tuple-element.8) | copy-start | bytes 983044

commit v3 on v1

--- a/solution.py
+++ b/solution.py
@@ -12,6 +12,10 @@
 SCALE = HEAD_DIM ** (-0.5)
 LOG2E = math.log2(math.e)
 LANES = 128
+RUN = 8
+DIRECT = 5
+LAG = 6
+ROUTES = (1, 2, 3)
 MESH = pl.DeviceIdType.MESH
 NT = (((1,), (1,)), ((), ()))
 NN = (((1,), (0,)), ((), ()))
@@ -26,9 +30,10 @@
     n_outer, n_inner, chunks,
     q_hbm, k_hbm, v_hbm, g_hbm, log_hbm, delta_hbm,
     dq_hbm, dk_hbm, dv_hbm,
-    qg, kv, stats, dq_own, dkv_own, dq_send, dkv_send, dq_recv, dkv_recv, out,
+    qg, kv, relay, stats, dq_own, dkv_own, dq_send, dkv_send, dq_recv, dkv_recv, out,
     stage_sem, stat_sem, qg_send_sem, qg_recv_sem, kv_send_sem, kv_recv_sem,
     st_send_sem, st_recv_sem, dq_send_sem, dq_recv_sem, dkv_send_sem, dkv_recv_sem, out_sem,
+    relay_send_sem, relay_recv_sem,
 ):
     o, i = lax.axis_index("outer"), lax.axis_index("inner")
     up = (lax.rem(o + 1, n_outer), i)
@@ -36,6 +41,34 @@
     right = (o, lax.rem(i + 1, n_inner))
     left = (o, lax.rem(i + n_inner - 1, n_inner))
 
+    place = lax.rem(i, RUN)
+    sends_keys, sends_sums = place == RUN - 1, place == 0
+    ends = jnp.logical_or(sends_keys, sends_sums)
+    relays = jnp.logical_not(ends)
+    relays_keys = jnp.logical_and(relays, lax.rem(place, 2) == 1)
+    relays_sums = jnp.logical_and(relays, lax.rem(place, 2) == 0)
+    odd_place = lax.rem(place, 2) == 1
+    route = (place + 1) // 2
+    units = (2 * chunks - DIRECT) // 3
+
+    def along(distance):
+        return (o, lax.rem(i + (distance + n_inner), n_inner))
+
+    def key_relay(k):
+        return along(2 * k - RUN)
+
+    def sum_relay(k):
+        return along(2 * k)
+
+    key_source, key_target = along(RUN - 2 * route), along(RUN + 1 - 2 * route)
+    sum_source, sum_target = along(-2 * route), along(-2 * route - 1)
+    partners = (
+        (sends_keys, [key_relay(k) for k in ROUTES] + [along(2 * k + 1) for k in ROUTES]),
+        (sends_sums, [sum_relay(k) for k in ROUTES] + [along(2 * k - RUN - 1) for k in ROUTES]),
+        (relays_keys, [key_source, key_target]),
+        (relays_sums, [sum_source, sum_target]),
+    )
+
     def columns(c):
         return pl.ds(pl.multiple_of(c * LANES, LANES), LANES)
 
@@ -58,6 +91,31 @@
     def send_kv(c):
         return remote(kv.at[c, 0], kv.at[c, 1], kv_send_sem.at[c], kv_recv_sem.at[c], right)
 
+    def send_kv_routes(c):
+        for n in range(2):
+            u = 2 * c + n
+
+            @pl.when(u < DIRECT)
+            def _():
+                remote(
+                    kv.at[c, 0, n], kv.at[c, 1, n], kv_send_sem.at[c], kv_recv_sem.at[c], right
+                ).start()
+
+            @pl.when(u >= DIRECT)
+            def _():
+                k, j = 1 + lax.rem(u - DIRECT + 3, 3), jnp.maximum(u - DIRECT, 0) // 3
+                remote(
+                    kv.at[c, 0, n], relay.at[j], kv_send_sem.at[c], relay_recv_sem.at[j], key_relay(k)
+                ).start()
+
+    def pass_kv(j):
+        u = DIRECT + 3 * j + route - 1
+        c, n = u // 2, lax.rem(u, 2)
+        return remote(relay.at[j], kv.at[c, 1, n], relay_send_sem.at[j], kv_recv_sem.at[c], key_target)
+
+    def arrived(j):
+        return remote(relay.at[j], relay.at[j], relay_send_sem.at[j], relay_recv_sem.at[j], right)
+
     def send_stats(n):
         return remote(stats.at[0, n], stats.at[1, n], st_send_sem.at[n], st_recv_sem.at[n], down)
 
@@ -66,6 +124,37 @@
 
     def send_dkv(c):
         return remote(dkv_send.at[c], dkv_recv.at[c], dkv_send_sem.at[c], dkv_recv_sem.at[c], left)
+
+    def send_dkv_routes(c):
+        for n in range(2):
+            u = 2 * c + n
+
+            @pl.when(u >= 2 * chunks - DIRECT)
+            def _():
+                remote(
+                    dkv_send.at[c, n], dkv_recv.at[c, n], dkv_send_sem.at[c], dkv_recv_sem.at[c], left
+                ).start()
+
+            @pl.when(u < 2 * chunks - DIRECT)
+            def _():
+                k, j = 1 + lax.rem(u, 3), jnp.minimum(u // 3, units - 1)
+                remote(
+                    dkv_send.at[c, n], relay.at[j], dkv_send_sem.at[c], relay_recv_sem.at[j], sum_relay(k)
+                ).start()
+
+    def pass_dkv(j):
+        u = 3 * j + route - 1
+        c, n = u // 2, lax.rem(u, 2)
+        return remote(relay.at[j], dkv_recv.at[c, n], relay_send_sem.at[j], dkv_recv_sem.at[c], sum_target)
+
+    def spread(condition, c, one, by_route):
+        @pl.when(condition)
+        def _():
+            by_route(c)
+
+        @pl.when(jnp.logical_not(condition))
+        def _():
+            one.start()
 
     def write(c):
         return [
@@ -88,7 +177,12 @@
     barrier = pltpu.get_barrier_semaphore()
     for device in (up, down, right, left):
         pl.semaphore_signal(barrier, inc=1, device_id=device, device_id_type=MESH)
-    pl.semaphore_wait(barrier, 4)
+    for role, devices in partners:
+        @pl.when(role)
+        def _():
+            for device in devices:
+                pl.semaphore_signal(barrier, inc=1, device_id=device, device_id_type=MESH)
+    pl.semaphore_wait(barrier, 6 + 4 * ends.astype(jnp.int32))
 
     for n, copy in enumerate(stat_copies):
         copy.wait()
@@ -98,8 +192,28 @@
     def _(c):
         for copy in stage(c):
             copy.wait()
-        send_qg(c).start()
-        send_kv(c).start()
+        spread(sends_keys, c, send_kv(c), send_kv_routes)
+
+        @pl.when(jnp.logical_not(odd_place))
+        def _():
+            send_qg(c).start()
+
+    @pl.when(relays_keys)
+    def _():
+        @pl.loop(0, units)
+        def _(j):
+            arrived(j).wait_recv()
+            pass_kv(j).start()
+
+    @pl.when(odd_place)
+    def _():
+        @pl.loop(0, chunks)
+        def _(c):
+            send_qg(c).start()
+
+    def pass_sums(j):
+        arrived(j).wait_recv()
+        pass_dkv(j).start()
 
     for n in range(2):
         send_stats(n).wait_recv()
@@ -108,6 +222,10 @@
 
     @pl.loop(0, chunks)
     def _(c):
+        @pl.when(jnp.logical_and(relays_sums, jnp.logical_and(lax.rem(c, 2) == 0, c >= LAG)))
+        def _():
+            pass_sums((c - LAG) // 2)
+
         send_qg(c).wait_recv()
         send_kv(c).wait_recv()
         queries = jnp.concatenate([qg[c, 0, 0], qg[c, 1, 0]], axis=0)
@@ -139,10 +257,16 @@
         send_dq(c).start()
         dkv_send[c, 0] = dk[rows:].astype(jnp.bfloat16)
         dkv_send[c, 1] = dv[rows:].astype(jnp.bfloat16)
-        send_dkv(c).start()
+        spread(sends_sums, c, send_dkv(c), send_dkv_routes)
         dq_own[c] = dq[:rows]
         dkv_own[c, 0] = dk[:rows]
         dkv_own[c, 1] = dv[:rows]
+
+    @pl.when(relays_sums)
+    def _():
+        @pl.loop((chunks - LAG) // 2, units)
+        def _(j):
+            pass_sums(j)
 
     @pl.loop(0, chunks)
     def _(c):
@@ -157,6 +281,12 @@
 
     for n in range(2):
         send_stats(n).wait_send()
+
+    @pl.when(relays)
+    def _():
+        @pl.loop(0, units)
+        def _(j):
+            arrived(j).wait_send()
 
     @pl.loop(0, chunks)
     def _(c):
@@ -185,6 +315,7 @@
         scratch_shapes=[
             pltpu.VMEM((chunks, 2, 2, rows, LANES), low),
             pltpu.VMEM((chunks, 2, 2, rows, LANES), low),
+            pltpu.VMEM((chunks // 2, rows, LANES), low),
             pltpu.VMEM((2, 2, heads, rows), full),
             pltpu.VMEM((chunks, rows, LANES), full),
             pltpu.VMEM((chunks, 2, rows, LANES), full),
@@ -198,9 +329,10 @@
             dma((2,)), dma((2,)),
             dma((chunks,)), dma((chunks,)), dma((chunks,)), dma((chunks,)),
             dma((chunks, 3)),
+            dma((chunks // 2,)), dma((chunks // 2,)),
         ],
         compiler_params=pltpu.CompilerParams(
-            collective_id=0, has_side_effects=True, vmem_limit_bytes=40 * 2**20
+            collective_id=0, has_side_effects=True, vmem_limit_bytes=60 * 2**20
         ),
         cost_estimate=pl.CostEstimate(
             flops=40 * rows * rows * width, bytes_accessed=14 * rows * width,

time: 62.2 us -> 55.4 us (0.89)
  the two profiles are of different devices: /device:TPU:7 before, /device:TPU:1 now
where the time goes in v3:
time: 55.4 us; the launch traced here: 55.1 us
  Pallas kernels  50.9 us (92%)
  local copies, waits for them, and re-layouts  3.58 us (6%)
  between operations  0.65 us (1%)
    pallas_call x1, Pallas kernels, body(): pl.pallas_call(functools.partial(kernel, lax.axis_size('outer'), lax.axis...  50.9 us
    unnamed x7, local copies, waits for them, and re-layouts  3.58 us

profile of v3, /device:TPU:1, one launch (start us, length us, event | category | flops | bytes accessed | tf_op | source)
XLA Modules:
  0.0 55.1 jit_solution(12881922507435222182)
XLA Ops:
  0.6 50.9 %window_backward.1 = (bf16[128,1280]{1,0:T(8,128)(2,1)}, bf16[128,1280]{1,0:T(8,128)(2,1)}, bf16[128,1280]{1,0:T(8,128)(2,1)}) custom-call(bf16[128,1280]{1,0:T(8,128)(2,1)} %q_hbm.1, bf16[128,1280]{1,0:T(8,128)(2,1)} %k_hbm.1, bf16[128,1280]{1,0:T(8,128)(2,1)} %v_hbm.1, bf16[128,1280]{1,0:T(8,128)(2,1)} %g_hbm.1, f32[20,128]{1,0:T(8,128)} %log_hbm.1, ...), custom_call_target="tpu_custom_call" | custom-call | flops 838860800 | bytes 2293760 | tf_op jit(solution)/shard_map/window_backward/pallas_call | solution.py:308
  51.5 0.0 copy-start.1
  51.6 1.8 %copy.12 = bf16[128,1280]{1,0:T(8,128)(2,1)} copy(bf16[128,1280]{1,0:T(8,128)(2,1)} %get-tuple-element.6) | data formatting | bytes 655360
  53.3 0.0 copy-done.1
  53.3 0.0 copy-start
  53.3 0.7 %copy.13 = bf16[128,1280]{1,0:T(8,128)(2,1)} copy(bf16[128,1280]{1,0:T(8,128)(2,1)S(1)} %copy-done.1) | data formatting | bytes 655360
  54.1 0.4 copy-done
  54.4 0.7 %copy.14 = bf16[128,1280]{1,0:T(8,128)(2,1)} copy(bf16[128,1280]{1,0:T(8,128)(2,1)S(1)} %copy-done) | data formatting | bytes 655360
Async XLA Ops:
  51.5 1.8 %copy-start.1 = (bf16[128,1280]{1,0:T(8,128)(2,1)S(1)}, bf16[128,1280]{1,0:T(8,128)(2,1)}, u32[]{:S(2)}) copy-start(bf16[128,1280]{1,0:T(8,128)(2,1)} %get-tuple-element.7) | copy-start | bytes 983044
  53.3 1.1 %copy-start = (bf16[128,1280]{1,0:T(8,128)(2,1)S(1)}, bf16[128,1280]{1,0:T(8,128)(2,1)}, u32[]{:S(2)}) copy-start(bf16[128,1280]{1,0:T(8,128)(2,1)} %get-tuple-element.8) | copy-start | bytes 983044

commit v4 on v3

--- a/solution.py
+++ b/solution.py
@@ -19,7 +19,6 @@
 MESH = pl.DeviceIdType.MESH
 NT = (((1,), (1,)), ((), ()))
 NN = (((1,), (0,)), ((), ()))
-TN = (((0,), (0,)), ((), ()))
 
 
 def mm(a, b, dims):
@@ -48,6 +47,8 @@
     relays_keys = jnp.logical_and(relays, lax.rem(place, 2) == 1)
     relays_sums = jnp.logical_and(relays, lax.rem(place, 2) == 0)
     odd_place = lax.rem(place, 2) == 1
+    rows = q_hbm.shape[0]
+    holds_dq = jnp.logical_and(lax.rem(o, 4) == 2, jnp.logical_not(odd_place))
     route = (place + 1) // 2
     units = (2 * chunks - DIRECT) // 3
 
@@ -218,7 +219,50 @@
     for n in range(2):
         send_stats(n).wait_recv()
 
-    first_head = lax.broadcasted_iota(jnp.int32, (1, LANES), 1) < HEAD_DIM
+    lanes = lax.broadcasted_iota(jnp.int32, (1, LANES), 1)
+    heads_of = (lanes < HEAD_DIM, lanes >= HEAD_DIM)
+
+    def stat(n, row):
+        return jnp.concatenate([stats[0, n, pl.ds(row, 1), :], stats[1, n, pl.ds(row, 1), :]], axis=1)
+
+    def terms(c, keys, values):
+        queries = jnp.concatenate([qg[c, 0, 0], qg[c, 1, 0]], axis=0)
+        grads = jnp.concatenate([qg[c, 0, 1], qg[c, 1, 1]], axis=0)
+        scores = [mm(jnp.where(mine, keys, jnp.zeros_like(keys)), queries, NT) for mine in heads_of]
+        dprobs = [mm(jnp.where(mine, values, jnp.zeros_like(values)), grads, NT) for mine in heads_of]
+        probs = [
+            jnp.exp2(scores[h] * (SCALE * LOG2E) - stat(0, 2 * c + h) * LOG2E) for h in range(2)
+        ]
+        score_grad = [
+            (probs[h] * (dprobs[h] - stat(1, 2 * c + h))).astype(jnp.bfloat16) for h in range(2)
+        ]
+        dv = [mm(part.astype(jnp.bfloat16), grads, NN) for part in probs]
+        dk = [mm(part, queries, NN) for part in score_grad]
+        keys_t = jnp.transpose(keys)
+        dq = [
+            mm(keys_t[h * HEAD_DIM:(h + 1) * HEAD_DIM], score_grad[h], NN) for h in range(2)
+        ]
+        return (
+            jnp.transpose(jnp.concatenate(dq, axis=0)) * SCALE,
+            jnp.where(heads_of[0], dk[0], dk[1]) * SCALE,
+            jnp.where(heads_of[0], dv[0], dv[1]),
+        )
+
+    def send_back(c, dq, dk_left, dv_left):
+        dq_send[c] = dq[rows:].astype(jnp.bfloat16)
+
+        @pl.when(jnp.logical_not(holds_dq))
+        def _():
+            send_dq(c).start()
+
+        dkv_send[c, 0] = dk_left.astype(jnp.bfloat16)
+        dkv_send[c, 1] = dv_left.astype(jnp.bfloat16)
+        spread(sends_sums, c, send_dkv(c), send_dkv_routes)
+        dq_own[c] = dq[:rows]
+
+    def keep(c, dk, dv):
+        dkv_own[c, 0] = dk
+        dkv_own[c, 1] = dv
 
     @pl.loop(0, chunks)
     def _(c):
@@ -228,45 +272,24 @@
 
         send_qg(c).wait_recv()
         send_kv(c).wait_recv()
-        queries = jnp.concatenate([qg[c, 0, 0], qg[c, 1, 0]], axis=0)
-        grads = jnp.concatenate([qg[c, 0, 1], qg[c, 1, 1]], axis=0)
+
         keys = jnp.concatenate([kv[c, 0, 0], kv[c, 1, 0]], axis=0)
         values = jnp.concatenate([kv[c, 0, 1], kv[c, 1, 1]], axis=0)
-        dq = None
-        dks, dvs = [], []
-        for head in range(2):
-            mine = first_head if head == 0 else jnp.logical_not(first_head)
-            row = 2 * c + head
-            logs = jnp.concatenate([stats[0, 0, pl.ds(row, 1), :], stats[1, 0, pl.ds(row, 1), :]], axis=1)
-            deltas = jnp.concatenate([stats[0, 1, pl.ds(row, 1), :], stats[1, 1, pl.ds(row, 1), :]], axis=1)
-            keys_h = jnp.where(mine, keys, jnp.zeros_like(keys))
-            values_h = jnp.where(mine, values, jnp.zeros_like(values))
-            scores = mm(keys_h, queries, NT)
-            probs = jnp.exp2(scores * (SCALE * LOG2E) - logs * LOG2E)
-            dprobs = mm(values_h, grads, NT)
-            score_grad = (probs * (dprobs - deltas)).astype(jnp.bfloat16)
-            dvs.append(mm(probs.astype(jnp.bfloat16), grads, NN))
-            dks.append(mm(score_grad, queries, NN))
-            part = mm(score_grad, keys_h, TN)
-            dq = part if dq is None else dq + part
-        dk = jnp.where(first_head, dks[0], dks[1]) * SCALE
-        dv = jnp.where(first_head, dvs[0], dvs[1])
-        dq = dq * SCALE
-        rows = dq.shape[0] // 2
-        dq_send[c] = dq[rows:].astype(jnp.bfloat16)
-        send_dq(c).start()
-        dkv_send[c, 0] = dk[rows:].astype(jnp.bfloat16)
-        dkv_send[c, 1] = dv[rows:].astype(jnp.bfloat16)
-        spread(sends_sums, c, send_dkv(c), send_dkv_routes)
-        dq_own[c] = dq[:rows]
-        dkv_own[c, 0] = dk[:rows]
-        dkv_own[c, 1] = dv[:rows]
+        dq, dk, dv = terms(c, keys, values)
+        send_back(c, dq, dk[rows:], dv[rows:])
+        keep(c, dk[:rows], dv[:rows])
 
     @pl.when(relays_sums)
     def _():
         @pl.loop((chunks - LAG) // 2, units)
         def _(j):
             pass_sums(j)
+
+    @pl.when(holds_dq)
+    def _():
+        @pl.loop(0, chunks)
+        def _(c):
+            send_dq(c).start()
 
     @pl.loop(0, chunks)
     def _(c):

time: 55.4 us -> 55.4 us (level)
  no operation moved by 1% of the time
where the time goes in v4:
time: 55.4 us; the launch traced here: 55.1 us
  Pallas kernels  50.9 us (92%)
  local copies, waits for them, and re-layouts  3.58 us (6%)
  between operations  0.65 us (1%)
    pallas_call x1, Pallas kernels, body(): pl.pallas_call(functools.partial(kernel, lax.axis_size('outer'), lax.axis...  50.9 us
    unnamed x7, local copies, waits for them, and re-layouts  3.58 us

profile of v4, /device:TPU:1, one launch (start us, length us, event | category | flops | bytes accessed | tf_op | source)
XLA Modules:
  0.0 55.1 jit_solution(6611626672471742379)
XLA Ops:
  0.6 50.9 %window_backward.1 = (bf16[128,1280]{1,0:T(8,128)(2,1)}, bf16[128,1280]{1,0:T(8,128)(2,1)}, bf16[128,1280]{1,0:T(8,128)(2,1)}) custom-call(bf16[128,1280]{1,0:T(8,128)(2,1)} %q_hbm.1, bf16[128,1280]{1,0:T(8,128)(2,1)} %k_hbm.1, bf16[128,1280]{1,0:T(8,128)(2,1)} %v_hbm.1, bf16[128,1280]{1,0:T(8,128)(2,1)} %g_hbm.1, f32[20,128]{1,0:T(8,128)} %log_hbm.1, ...), custom_call_target="tpu_custom_call" | custom-call | flops 838860800 | bytes 2293760 | tf_op jit(solution)/shard_map/window_backward/pallas_call | solution.py:331
  51.5 0.0 copy-start.1
  51.6 1.8 %copy.12 = bf16[128,1280]{1,0:T(8,128)(2,1)} copy(bf16[128,1280]{1,0:T(8,128)(2,1)} %get-tuple-element.6) | data formatting | bytes 655360
  53.3 0.0 copy-done.1
  53.3 0.0 copy-start
  53.3 0.7 %copy.13 = bf16[128,1280]{1,0:T(8,128)(2,1)} copy(bf16[128,1280]{1,0:T(8,128)(2,1)S(1)} %copy-done.1) | data formatting | bytes 655360
  54.1 0.4 copy-done
  54.4 0.7 %copy.14 = bf16[128,1280]{1,0:T(8,128)(2,1)} copy(bf16[128,1280]{1,0:T(8,128)(2,1)S(1)} %copy-done) | data formatting | bytes 655360
Async XLA Ops:
  51.5 1.8 %copy-start.1 = (bf16[128,1280]{1,0:T(8,128)(2,1)S(1)}, bf16[128,1280]{1,0:T(8,128)(2,1)}, u32[]{:S(2)}) copy-start(bf16[128,1280]{1,0:T(8,128)(2,1)} %get-tuple-element.7) | copy-start | bytes 983044
  53.3 1.1 %copy-start = (bf16[128,1280]{1,0:T(8,128)(2,1)S(1)}, bf16[128,1280]{1,0:T(8,128)(2,1)}, u32[]{:S(2)}) copy-start(bf16[128,1280]{1,0:T(8,128)(2,1)} %get-tuple-element.8) | copy-start | bytes 983044

commit v5 on v4

--- a/solution.py
+++ b/solution.py
@@ -15,6 +15,7 @@
 RUN = 8
 DIRECT = 5
 LAG = 6
+AHEAD = 4
 ROUTES = (1, 2, 3)
 MESH = pl.DeviceIdType.MESH
 NT = (((1,), (1,)), ((), ()))
@@ -32,7 +33,7 @@
     qg, kv, relay, stats, dq_own, dkv_own, dq_send, dkv_send, dq_recv, dkv_recv, out,
     stage_sem, stat_sem, qg_send_sem, qg_recv_sem, kv_send_sem, kv_recv_sem,
     st_send_sem, st_recv_sem, dq_send_sem, dq_recv_sem, dkv_send_sem, dkv_recv_sem, out_sem,
-    relay_send_sem, relay_recv_sem,
+    relay_send_sem, relay_recv_sem, row_sem,
 ):
     o, i = lax.axis_index("outer"), lax.axis_index("inner")
     up = (lax.rem(o + 1, n_outer), i)
@@ -52,6 +53,9 @@
     route = (place + 1) // 2
     units = (2 * chunks - DIRECT) // 3
 
+    first_row, last_row = o == 0, o == n_outer - 1
+    ahead = jnp.where(last_row, AHEAD, chunks)
+
     def along(distance):
         return (o, lax.rem(i + (distance + n_inner), n_inner))
 
@@ -176,18 +180,31 @@
             copy.start()
 
     barrier = pltpu.get_barrier_semaphore()
-    for device in (up, down, right, left):
+    for device in (down, right, left):
         pl.semaphore_signal(barrier, inc=1, device_id=device, device_id_type=MESH)
+
+    @pl.when(jnp.logical_not(last_row))
+    def _():
+        pl.semaphore_signal(barrier, inc=1, device_id=up, device_id_type=MESH)
+
     for role, devices in partners:
         @pl.when(role)
         def _():
             for device in devices:
                 pl.semaphore_signal(barrier, inc=1, device_id=device, device_id_type=MESH)
-    pl.semaphore_wait(barrier, 6 + 4 * ends.astype(jnp.int32))
+    pl.semaphore_wait(barrier, 6 + 4 * ends.astype(jnp.int32) - first_row.astype(jnp.int32))
+
+    @pl.when(last_row)
+    def _():
+        pl.semaphore_signal(row_sem, inc=1, device_id=up, device_id_type=MESH)
 
     for n, copy in enumerate(stat_copies):
         copy.wait()
-        send_stats(n).start()
+
+        @pl.when(jnp.logical_not(first_row))
+        def _():
+            send_stats(n).start()
+
 
     @pl.loop(0, chunks)
     def _(c):
@@ -195,7 +212,7 @@
             copy.wait()
         spread(sends_keys, c, send_kv(c), send_kv_routes)
 
-        @pl.when(jnp.logical_not(odd_place))
+        @pl.when(jnp.logical_and(jnp.logical_not(jnp.logical_or(odd_place, first_row)), c < ahead))
         def _():
             send_qg(c).start()
 
@@ -206,9 +223,15 @@
             arrived(j).wait_recv()
             pass_kv(j).start()
 
-    @pl.when(odd_place)
-    def _():
-        @pl.loop(0, chunks)
+    @pl.when(first_row)
+    def _():
+        pl.semaphore_wait(row_sem, 1)
+        for n in range(2):
+            send_stats(n).start()
+
+    @pl.when(jnp.logical_or(odd_place, first_row))
+    def _():
+        @pl.loop(0, ahead)
         def _(c):
             send_qg(c).start()
 
@@ -272,6 +295,10 @@
 
         send_qg(c).wait_recv()
         send_kv(c).wait_recv()
+
+        @pl.when(c + ahead < chunks)
+        def _():
+            send_qg(jnp.minimum(c + ahead, chunks - 1)).start()
 
         keys = jnp.concatenate([kv[c, 0, 0], kv[c, 1, 0]], axis=0)
         values = jnp.concatenate([kv[c, 0, 1], kv[c, 1, 1]], axis=0)
@@ -352,7 +379,7 @@
             dma((2,)), dma((2,)),
             dma((chunks,)), dma((chunks,)), dma((chunks,)), dma((chunks,)),
             dma((chunks, 3)),
-            dma((chunks // 2,)), dma((chunks // 2,)),
+            dma((chunks // 2,)), dma((chunks // 2,)), pltpu.SemaphoreType.REGULAR,
         ],
         compiler_params=pltpu.CompilerParams(
             collective_id=0, has_side_effects=True, vmem_limit_bytes=60 * 2**20

time: 55.4 us -> 53.7 us (0.969)
  Pallas kernels: 50.9 us -> 49.2 us
    pallas_call x1, Pallas kernels: 50.9 us -> 49.2 us  [body(): pl.pallas_call(functools.partial(kernel, lax.axis_size('outer'), lax.axis...]
where the time goes in v5:
time: 53.7 us; the launch traced here: 53.4 us
  Pallas kernels  49.2 us (92%)
  local copies, waits for them, and re-layouts  3.58 us (7%)
  between operations  0.65 us (1%)
    pallas_call x1, Pallas kernels, body(): pl.pallas_call(functools.partial(kernel, lax.axis_size('outer'), lax.axis...  49.2 us
    unnamed x7, local copies, waits for them, and re-layouts  3.58 us

profile of v5, /device:TPU:1, one launch (start us, length us, event | category | flops | bytes accessed | tf_op | source)
XLA Modules:
  0.0 53.4 jit_solution(14339141111809698048)
XLA Ops:
  0.6 49.2 %window_backward.1 = (bf16[128,1280]{1,0:T(8,128)(2,1)}, bf16[128,1280]{1,0:T(8,128)(2,1)}, bf16[128,1280]{1,0:T(8,128)(2,1)}) custom-call(bf16[128,1280]{1,0:T(8,128)(2,1)} %q_hbm.1, bf16[128,1280]{1,0:T(8,128)(2,1)} %k_hbm.1, bf16[128,1280]{1,0:T(8,128)(2,1)} %v_hbm.1, bf16[128,1280]{1,0:T(8,128)(2,1)} %g_hbm.1, f32[20,128]{1,0:T(8,128)} %log_hbm.1, ...), custom_call_target="tpu_custom_call" | custom-call | flops 838860800 | bytes 2293760 | tf_op jit(solution)/shard_map/window_backward/pallas_call | solution.py:358
  49.8 0.0 copy-start.1
  49.8 1.8 %copy.12 = bf16[128,1280]{1,0:T(8,128)(2,1)} copy(bf16[128,1280]{1,0:T(8,128)(2,1)} %get-tuple-element.6) | data formatting | bytes 655360
  51.6 0.0 copy-done.1
  51.6 0.0 copy-start
  51.6 0.7 %copy.13 = bf16[128,1280]{1,0:T(8,128)(2,1)} copy(bf16[128,1280]{1,0:T(8,128)(2,1)S(1)} %copy-done.1) | data formatting | bytes 655360
  52.3 0.4 copy-done
  52.7 0.7 %copy.14 = bf16[128,1280]{1,0:T(8,128)(2,1)} copy(bf16[128,1280]{1,0:T(8,128)(2,1)S(1)} %copy-done) | data formatting | bytes 655360
Async XLA Ops:
  49.8 1.8 %copy-start.1 = (bf16[128,1280]{1,0:T(8,128)(2,1)S(1)}, bf16[128,1280]{1,0:T(8,128)(2,1)}, u32[]{:S(2)}) copy-start(bf16[128,1280]{1,0:T(8,128)(2,1)} %get-tuple-element.7) | copy-start | bytes 983044
  51.6 1.1 %copy-start = (bf16[128,1280]{1,0:T(8,128)(2,1)S(1)}, bf16[128,1280]{1,0:T(8,128)(2,1)}, u32[]{:S(2)}) copy-start(bf16[128,1280]{1,0:T(8,128)(2,1)} %get-tuple-element.8) | copy-start | bytes 983044

commit v6 on v5

--- a/solution.py
+++ b/solution.py
@@ -29,10 +29,10 @@
 def kernel(
     n_outer, n_inner, chunks,
     q_hbm, k_hbm, v_hbm, g_hbm, log_hbm, delta_hbm,
-    dq_hbm, dk_hbm, dv_hbm,
-    qg, kv, relay, stats, dq_own, dkv_own, dq_send, dkv_send, dq_recv, dkv_recv, out,
+    dq_out, dk_out, dv_out,
+    qg, kv, relay, stats, dq_own, dkv_own, dq_send, dkv_send, dq_recv, dkv_recv,
     stage_sem, stat_sem, qg_send_sem, qg_recv_sem, kv_send_sem, kv_recv_sem,
-    st_send_sem, st_recv_sem, dq_send_sem, dq_recv_sem, dkv_send_sem, dkv_recv_sem, out_sem,
+    st_send_sem, st_recv_sem, dq_send_sem, dq_recv_sem, dkv_send_sem, dkv_recv_sem,
     relay_send_sem, relay_recv_sem, row_sem,
 ):
     o, i = lax.axis_index("outer"), lax.axis_index("inner")
@@ -160,12 +160,6 @@
         @pl.when(jnp.logical_not(condition))
         def _():
             one.start()
-
-    def write(c):
-        return [
-            pltpu.make_async_copy(out.at[n, c], dst.at[:, columns(c)], out_sem.at[c, n])
-            for n, dst in enumerate((dq_hbm, dk_hbm, dv_hbm))
-        ]
 
     stat_copies = [
         pltpu.make_async_copy(src, stats.at[0, n], stat_sem.at[n])
@@ -321,13 +315,11 @@
     @pl.loop(0, chunks)
     def _(c):
         send_dq(c).wait_recv()
-        out[0, c] = (dq_own[c] + dq_recv[c].astype(jnp.float32)).astype(jnp.bfloat16)
+        dq_out[:, columns(c)] = (dq_own[c] + dq_recv[c].astype(jnp.float32)).astype(jnp.bfloat16)
         send_dkv(c).wait_recv()
-        for n in range(2):
+        for n, ref in enumerate((dk_out, dv_out)):
             total = dkv_own[c, n] + dkv_recv[c, n].astype(jnp.float32)
-            out[1 + n, c] = total.astype(jnp.bfloat16)
-        for copy in write(c):
-            copy.start()
+            ref[:, columns(c)] = total.astype(jnp.bfloat16)
 
     for n in range(2):
         send_stats(n).wait_send()
@@ -344,8 +336,6 @@
         send_kv(c).wait_send()
         send_dq(c).wait_send()
         send_dkv(c).wait_send()
-        for copy in write(c):
-            copy.wait()
 
 
 def body(queries, key_states, value_states, out_grad, log_total, row_delta):
@@ -354,14 +344,14 @@
     chunks = width // LANES
     dma = pltpu.SemaphoreType.DMA
     low, full = jnp.bfloat16, jnp.float32
-    block = jax.ShapeDtypeStruct((rows, width), low)
+    block = pltpu.VMEM((rows, width), low)
     return pl.pallas_call(
         functools.partial(
             kernel, lax.axis_size("outer"), lax.axis_size("inner"), chunks
         ),
         out_shape=(block, block, block),
         in_specs=[pl.BlockSpec(memory_space=pl.ANY)] * 6,
-        out_specs=[pl.BlockSpec(memory_space=pl.ANY)] * 3,
+        out_specs=[pl.BlockSpec(memory_space=pltpu.VMEM)] * 3,
         scratch_shapes=[
             pltpu.VMEM((chunks, 2, 2, rows, LANES), low),
             pltpu.VMEM((chunks, 2, 2, rows, LANES), low),
@@ -373,23 +363,24 @@
             pltpu.VMEM((chunks, 2, rows, LANES), low),
             pltpu.VMEM((chunks, rows, LANES), low),
             pltpu.VMEM((chunks, 2, rows, LANES), low),
-            pltpu.VMEM((3, chunks, rows, LANES), low),
             dma((chunks, 4)), dma((2,)),
             dma((chunks,)), dma((chunks,)), dma((chunks,)), dma((chunks,)),
             dma((2,)), dma((2,)),
             dma((chunks,)), dma((chunks,)), dma((chunks,)), dma((chunks,)),
-            dma((chunks, 3)),
             dma((chunks // 2,)), dma((chunks // 2,)), pltpu.SemaphoreType.REGULAR,
         ],
         compiler_params=pltpu.CompilerParams(
-            collective_id=0, has_side_effects=True, vmem_limit_bytes=60 * 2**20
+            collective_id=0, has_side_effects=True, vmem_limit_bytes=32 * 2**20
         ),
         cost_estimate=pl.CostEstimate(
             flops=40 * rows * rows * width, bytes_accessed=14 * rows * width,
             transcendentals=4 * heads * rows * rows,
         ),
         name="window_backward",
-    )(queries, key_states, value_states, out_grad, log_total, row_delta)
+    )(*(
+        pltpu.with_memory_space_constraint(array, pltpu.HBM)
+        for array in (queries, key_states, value_states, out_grad, log_total, row_delta)
+    ))
 
 
 def solution(mesh):

time: 53.7 us -> 51.4 us (0.957)
  local copies, waits for them, and re-layouts: 3.58 us -> 2.17 us
  Pallas kernels: 49.2 us -> 48.4 us
    unnamed x7 -> x3, local copies, waits for them, and re-layouts: 3.58 us -> 2.17 us
    pallas_call x1, Pallas kernels: 49.2 us -> 48.4 us  [body(): pl.pallas_call(functools.partial(kernel, lax.axis_size('outer'), lax.axis...]
where the time goes in v6:
time: 51.4 us; the launch traced here: 51.2 us
  Pallas kernels  48.4 us (94%)
  local copies, waits for them, and re-layouts  2.17 us (4%)
  between operations  0.64 us (1%)
    pallas_call x1, Pallas kernels, body(): pl.pallas_call(functools.partial(kernel, lax.axis_size('outer'), lax.axis...  48.4 us
    unnamed x3, local copies, waits for them, and re-layouts  2.17 us

profile of v6, /device:TPU:1, one launch (start us, length us, event | category | flops | bytes accessed | tf_op | source)
XLA Modules:
  0.0 51.2 jit_solution(12043488319197744321)
XLA Ops:
  0.6 48.4 %window_backward.1 = (bf16[128,1280]{1,0:T(8,128)(2,1)S(1)}, bf16[128,1280]{1,0:T(8,128)(2,1)S(1)}, bf16[128,1280]{1,0:T(8,128)(2,1)S(1)}) custom-call(bf16[128,1280]{1,0:T(8,128)(2,1)} %q_hbm.1, bf16[128,1280]{1,0:T(8,128)(2,1)} %k_hbm.1, bf16[128,1280]{1,0:T(8,128)(2,1)} %v_hbm.1, bf16[128,1280]{1,0:T(8,128)(2,1)} %g_hbm.1, f32[20,128]{1,0:T(8,128)} %log_hbm.1, ...), custom_call_target="tpu_custom_call" | custom-call | flops 838860800 | bytes 2293760 | tf_op jit(solution)/shard_map/window_backward/pallas_call | solution.py:348
  49.0 0.7 %copy.12 = bf16[128,1280]{1,0:T(8,128)(2,1)} copy(bf16[128,1280]{1,0:T(8,128)(2,1)S(1)} %get-tuple-element.3) | data formatting | bytes 655360
  49.7 0.7 %copy.13 = bf16[128,1280]{1,0:T(8,128)(2,1)} copy(bf16[128,1280]{1,0:T(8,128)(2,1)S(1)} %get-tuple-element.4) | data formatting | bytes 655360
  50.5 0.7 %copy.14 = bf16[128,1280]{1,0:T(8,128)(2,1)} copy(bf16[128,1280]{1,0:T(8,128)(2,1)S(1)} %get-tuple-element.5) | data formatting | bytes 655360

commit v7 on v6

--- a/solution.py
+++ b/solution.py
@@ -15,7 +15,7 @@
 RUN = 8
 DIRECT = 5
 LAG = 6
-AHEAD = 4
+AHEAD = 3
 ROUTES = (1, 2, 3)
 MESH = pl.DeviceIdType.MESH
 NT = (((1,), (1,)), ((), ()))
@@ -338,6 +338,17 @@
         send_dkv(c).wait_send()
 
 
+def hand_over(dq, dk, dv, dq_out, dk_out, dv_out, sem):
+    copies = [
+        pltpu.make_async_copy(src, dst, sem.at[n])
+        for n, (src, dst) in enumerate(((dq, dq_out), (dk, dk_out), (dv, dv_out)))
+    ]
+    for copy in copies:
+        copy.start()
+    for copy in copies:
+        copy.wait()
+
+
 def body(queries, key_states, value_states, out_grad, log_total, row_delta):
     rows, width = queries.shape
     heads = log_total.shape[0]
@@ -345,7 +356,7 @@
     dma = pltpu.SemaphoreType.DMA
     low, full = jnp.bfloat16, jnp.float32
     block = pltpu.VMEM((rows, width), low)
-    return pl.pallas_call(
+    grads = pl.pallas_call(
         functools.partial(
             kernel, lax.axis_size("outer"), lax.axis_size("inner"), chunks
         ),
@@ -381,6 +392,14 @@
         pltpu.with_memory_space_constraint(array, pltpu.HBM)
         for array in (queries, key_states, value_states, out_grad, log_total, row_delta)
     ))
+    return pl.pallas_call(
+        hand_over,
+        out_shape=[pltpu.HBM((rows, width), low)] * 3,
+        in_specs=[pl.BlockSpec(memory_space=pltpu.VMEM)] * 3,
+        out_specs=[pl.BlockSpec(memory_space=pltpu.HBM)] * 3,
+        scratch_shapes=[dma((3,))],
+        name="hand_over",
+    )(*(pltpu.with_memory_space_constraint(array, pltpu.VMEM) for array in grads))
 
 
 def solution(mesh):

time: 51.4 us -> 50 us (0.973)
  the two profiles are of different devices: /device:TPU:1 before, /device:TPU:2 now
where the time goes in v7:
time: 50 us; the launch traced here: 49.7 us
  Pallas kernels  49.1 us (98%)
  between operations  0.64 us (1%)
    pallas_call x1, Pallas kernels, body(): pl.pallas_call(functools.partial(kernel, lax.axis_size('outer'), lax.axis...  48.1 us

profile of v7, /device:TPU:2, one launch (start us, length us, event | category | flops | bytes accessed | tf_op | source)
XLA Modules:
  0.0 49.7 jit_solution(15414169597068625992)
XLA Ops:
  0.6 48.1 %window_backward.1 = (bf16[128,1280]{1,0:T(8,128)(2,1)S(1)}, bf16[128,1280]{1,0:T(8,128)(2,1)S(1)}, bf16[128,1280]{1,0:T(8,128)(2,1)S(1)}) custom-call(bf16[128,1280]{1,0:T(8,128)(2,1)} %q_hbm.1, bf16[128,1280]{1,0:T(8,128)(2,1)} %k_hbm.1, bf16[128,1280]{1,0:T(8,128)(2,1)} %v_hbm.1, bf16[128,1280]{1,0:T(8,128)(2,1)} %g_hbm.1, f32[20,128]{1,0:T(8,128)} %log_hbm.1, ...), custom_call_target="tpu_custom_call" | custom-call | flops 838860800 | bytes 2293760 | tf_op jit(solution)/shard_map/window_backward/pallas_call | solution.py:359
  48.8 1.0 %hand_over.1 = (bf16[128,1280]{1,0:T(8,128)(2,1)}, bf16[128,1280]{1,0:T(8,128)(2,1)}, bf16[128,1280]{1,0:T(8,128)(2,1)}) custom-call(bf16[128,1280]{1,0:T(8,128)(2,1)S(1)} %get-tuple-element.6.dq, bf16[128,1280]{1,0:T(8,128)(2,1)S(1)} %get-tuple-element.7.dk, bf16[128,1280]{1,0:T(8,128)(2,1)S(1)} %get-tuple-element.8.dv), custom_call_target="tpu_custom_call" | custom-call | tf_op jit(solution)/shard_map/hand_over/pallas_call | solution.py:395

commit v8 on v7

--- a/solution.py
+++ b/solution.py
@@ -14,7 +14,7 @@
 LANES = 128
 RUN = 8
 DIRECT = 5
-LAG = 6
+LAG = 8
 AHEAD = 3
 ROUTES = (1, 2, 3)
 MESH = pl.DeviceIdType.MESH

time: 50 us -> 49.7 us (level)
  the two profiles are of different devices: /device:TPU:2 before, /device:TPU:7 now
where the time goes in v8:
time: 49.7 us; the launch traced here: 49.5 us
  Pallas kernels  48.8 us (98%)
  between operations  0.64 us (1%)
    pallas_call x1, Pallas kernels, body(): pl.pallas_call(functools.partial(kernel, lax.axis_size('outer'), lax.axis...  47.9 us

profile of v8, /device:TPU:7, one launch (start us, length us, event | category | flops | bytes accessed | tf_op | source)
XLA Modules:
  0.0 49.5 jit_solution(16817430516047373936)
XLA Ops:
  0.6 47.9 %window_backward.1 = (bf16[128,1280]{1,0:T(8,128)(2,1)S(1)}, bf16[128,1280]{1,0:T(8,128)(2,1)S(1)}, bf16[128,1280]{1,0:T(8,128)(2,1)S(1)}) custom-call(bf16[128,1280]{1,0:T(8,128)(2,1)} %q_hbm.1, bf16[128,1280]{1,0:T(8,128)(2,1)} %k_hbm.1, bf16[128,1280]{1,0:T(8,128)(2,1)} %v_hbm.1, bf16[128,1280]{1,0:T(8,128)(2,1)} %g_hbm.1, f32[20,128]{1,0:T(8,128)} %log_hbm.1, ...), custom_call_target="tpu_custom_call" | custom-call | flops 838860800 | bytes 2293760 | tf_op jit(solution)/shard_map/window_backward/pallas_call | solution.py:359
  48.5 1.0 %hand_over.1 = (bf16[128,1280]{1,0:T(8,128)(2,1)}, bf16[128,1280]{1,0:T(8,128)(2,1)}, bf16[128,1280]{1,0:T(8,128)(2,1)}) custom-call(bf16[128,1280]{1,0:T(8,128)(2,1)S(1)} %get-tuple-element.6.dq, bf16[128,1280]{1,0:T(8,128)(2,1)S(1)} %get-tuple-element.7.dk, bf16[128,1280]{1,0:T(8,128)(2,1)S(1)} %get-tuple-element.8.dv), custom_call_target="tpu_custom_call" | custom-call | tf_op jit(solution)/shard_map/hand_over/pallas_call | solution.py:395
